TPU v7x, 32 devices: a whole 2x2x4 slice. The times are simulated.
32 devices in a mesh: groups: 2 (over x), seq: 16 (over z, y, core).
Axes of the slice: x: 2, y: 2, z: 4, core: 2. Of those that a mesh axis runs over, the one named last changes fastest.
Arguments:
- prompt_query: bfloat16 [4096, 4096], P(('groups', 'seq')), parts along dimension 0, may hold values from -16 to 16
- prompt_key: bfloat16 [4096, 4096], P(('groups', 'seq')), parts along dimension 0, may hold values from -16 to 16
- prompt_value: bfloat16 [4096, 4096], P(('groups', 'seq')), parts along dimension 0, may hold values from -6 to 6
- response_embed: bfloat16 [1024, 4096], P('groups'), parts along dimension 0, may hold values from -32 to 32
- mask_embed: bfloat16 [4096], replicated, may hold values from -6 to 6
- commit_step: int32 [1024], P('groups'), parts along dimension 0, may hold values from 1 to 4
- block_index: int32 [2], P('groups'), parts along dimension 0, may hold values from 0 to 7
- attention_gain: bfloat16 [4096], replicated, may hold values from 0.099609375 to 1.8984375
- residual_gain: bfloat16 [4096], replicated, may hold values from 0.099609375 to 1.8984375
- query_weight: bfloat16 [4096, 4096], P(None, 'seq'), may hold values from -0.125 to 0.125
- key_weight: bfloat16 [4096, 4096], P(None, 'seq'), may hold values from -0.09375 to 0.09375
- value_weight: bfloat16 [4096, 4096], P(None, 'seq'), may hold values from -1.5 to 1.5
- output_weight: bfloat16 [4096, 4096], P('seq'), may hold values from -0.09375 to 0.09375
Outputs:
- prompt_context: bfloat16 [4096, 4096], P(('groups', 'seq')), parts along dimension 0
- response_residual: bfloat16 [4, 1024, 4096], P(None, ('groups', 'seq')), parts along dimension 1
- response_normed: bfloat16 [4, 1024, 4096], P(None, ('groups', 'seq')), parts along dimension 1
There are 2 independent parts, one for each index of `groups`. A program takes and returns all parts, laid end to end along the dimension named above; an argument that names none is the same for every part. Nothing has to cross between parts.
All inputs are finite; a program needn't handle non-finite values.
Results may differ from a plain program's by a relative error of at most 0.018.
Values may be sent and summed in bfloat16 or wider, within the bound.
A program may use at most 128 MiB of HBM per device.

v0:
```python
import functools
import math

import jax
import jax.numpy as jnp
from jax import lax
from jax.experimental import pallas as pl
from jax.experimental.pallas import tpu as pltpu
from jax.sharding import PartitionSpec as P

HD = 128
STEPS = 4
ROPE_BASE = 500000.0
NORM_EPS = 1e-05
QBLOCK = 256
VMEM_LIMIT = 48 * 1024 * 1024
NT = (((1,), (1,)), ((), ()))


def rope_tables(positions):
    half = HD // 2
    exponent = jnp.arange(half, dtype=jnp.float32) * (2.0 / HD)
    inv_freq = ROPE_BASE ** (-exponent)
    angles = positions.astype(jnp.float32)[:, None] * inv_freq[None, :]
    cosine = jnp.cos(angles)
    sine = jnp.sin(angles)
    return jnp.concatenate([cosine, cosine], axis=-1), jnp.concatenate([-sine, sine], axis=-1)


def rms_scale(row_values, gain_row):
    return (
        row_values
        * lax.rsqrt(jnp.mean(row_values * row_values, axis=-1, keepdims=True) + NORM_EPS)
        * gain_row.astype(jnp.float32)
    )


def rope_in(x, cosine, sine):
    return x * cosine + pltpu.roll(x, HD // 2, 1) * sine


def query_factor():
    return math.log2(math.e) / math.sqrt(HD)


def kv_prep_kernel(key_ref, value_ref, cos_ref, sin_ref, kv_ref):
    for h in range(key_ref.shape[1] // HD):
        cols = slice(h * HD, (h + 1) * HD)
        kv_ref[0, 0, :, cols] = rope_in(
            key_ref[:, cols].astype(jnp.float32), cos_ref[...], sin_ref[...]
        ).astype(jnp.bfloat16)
    kv_ref[0, 1] = value_ref[...]


def q_prep_kernel(query_ref, cos_ref, sin_ref, q_ref):
    for h in range(query_ref.shape[1] // HD):
        cols = slice(h * HD, (h + 1) * HD)
        turned = rope_in(query_ref[:, cols].astype(jnp.float32), cos_ref[...], sin_ref[...])
        q_ref[0, :, cols] = (turned * query_factor()).astype(jnp.bfloat16)


def response_kernel(
    q_ref, k_ref, v_ref, kv_ref, cos_ref, sin_ref, commit_ref,
    out_ref, key0_ref, value0_ref,
    q_both, k_both, v_both, prompt_va, step_va, part_o, part_m,
):
    resp = cos_ref.shape[0]
    shards, _, rows, _ = kv_ref.shape
    prompt = shards * rows
    cosine, sine = cos_ref[...], sin_ref[...]

    def both(ref, dest, turn, factor):
        shown = ref[pl.ds(0, resp), :]
        hidden = jnp.broadcast_to(ref[pl.ds(resp, 1), :], (resp, HD))
        for slot, x in ((0, hidden), (1, shown)):
            if turn:
                x = rope_in(x, cosine, sine)
            dest[pl.ds(slot * resp, resp), :] = (x * factor).astype(jnp.bfloat16).astype(jnp.float32)

    both(q_ref, q_both, True, query_factor())
    both(k_ref, k_both, True, 1.0)
    both(v_ref, v_both, False, 1.0)
    prompt_va[:, :HD] = kv_ref[:, 1].reshape(prompt, HD)
    prompt_va[:, HD:] = jnp.ones((prompt, HD), jnp.bfloat16)
    step_va[:, HD:] = jnp.ones((resp, HD), jnp.bfloat16)
    block = math.gcd(QBLOCK, resp)

    def prompt_part(i, carry):
        at = pl.ds(pl.multiple_of(i * block, block), block)
        q = q_both[at, :].astype(jnp.bfloat16)
        k = kv_ref[:, 0].reshape(prompt, HD)
        s = lax.dot_general(q, k, NT, preferred_element_type=jnp.float32)
        m = jnp.max(s, axis=-1, keepdims=True)
        p = jnp.exp2(s - m).astype(jnp.bfloat16)
        part_o[at, :] = jnp.dot(p, prompt_va[...], preferred_element_type=jnp.float32)
        part_m[at, :] = jnp.broadcast_to(m, (block, HD))
        return carry

    lax.fori_loop(0, 2 * resp // block, prompt_part, 0)
    out_rows = out_ref.shape[2]
    for step in range(STEPS):
        shown = commit_ref[...] <= step
        k_s = jnp.where(shown, k_both[resp:, :], k_both[:resp, :]).astype(jnp.bfloat16)
        v_s = jnp.where(shown, v_both[resp:, :], v_both[:resp, :]).astype(jnp.bfloat16)
        step_va[:, :HD] = v_s
        if step == 0:
            key0_ref[...] = k_s
            value0_ref[...] = v_s
        for i in range(resp // block):
            lo, hi = i * block, (i + 1) * block
            here = commit_ref[lo:hi, :] <= step

            def pick(ref):
                return jnp.where(here, ref[resp + lo : resp + hi, :HD], ref[lo:hi, :HD])

            q = pick(q_both).astype(jnp.bfloat16)
            s = lax.dot_general(q, k_s, NT, preferred_element_type=jnp.float32)
            m_prompt = pick(part_m)
            m = jnp.maximum(jnp.max(s, axis=-1, keepdims=True), m_prompt)
            p = jnp.exp2(s - m[:, :1]).astype(jnp.bfloat16)
            o = jnp.dot(p, step_va[...], preferred_element_type=jnp.float32)
            shrink = jnp.exp2(m_prompt - m)
            top = o[:, :HD] + shrink * pick(part_o)
            total = o[:, HD:] + shrink * jnp.where(
                here, part_o[resp + lo : resp + hi, HD:], part_o[lo:hi, HD:]
            )
            out_ref[lo // out_rows : hi // out_rows, step] = (
                (top / total).astype(jnp.bfloat16).reshape(block // out_rows, out_rows, HD)
            )


def prompt_kernel(q_ref, kv_ref, key0_ref, value0_ref, out_ref, va):
    shards, _, rows, _ = kv_ref.shape
    prompt = shards * rows

    @pl.when(pl.program_id(1) == 0)
    def _():
        va[:prompt, :HD] = kv_ref[:, 1].reshape(prompt, HD)
        va[prompt:, :HD] = value0_ref[...]
        va[:, HD:] = jnp.ones((va.shape[0], HD), jnp.bfloat16)

    q = q_ref[...].reshape(-1, HD)
    s1 = lax.dot_general(
        q, kv_ref[:, 0].reshape(prompt, HD), NT, preferred_element_type=jnp.float32
    )
    s2 = lax.dot_general(q, key0_ref[...], NT, preferred_element_type=jnp.float32)
    m = jnp.maximum(jnp.max(s1, axis=-1, keepdims=True), jnp.max(s2, axis=-1, keepdims=True))
    p1 = jnp.exp2(s1 - m).astype(jnp.bfloat16)
    p2 = jnp.exp2(s2 - m).astype(jnp.bfloat16)
    o = jnp.dot(p1, va[:prompt, :], preferred_element_type=jnp.float32)
    o += jnp.dot(p2, va[prompt:, :], preferred_element_type=jnp.float32)
    out_ref[...] = (o[:, :HD] / o[:, HD:]).astype(jnp.bfloat16).reshape(out_ref.shape)


def per_device(
    prompt_query, prompt_key, prompt_value, response_embed, mask_embed, commit_step, block_index,
    attention_gain, residual_gain, query_weight, key_weight, value_weight, output_weight,
):
    rows, width = prompt_query.shape
    resp = response_embed.shape[0]
    model = response_embed.shape[1]
    shards = lax.axis_size("seq")
    groups = lax.axis_size("groups")
    me = lax.axis_index("seq")
    group = lax.axis_index("groups")
    cores = 2
    core = lax.rem(me, cores)
    local = query_weight.shape[1]
    heads = local // HD
    prompt = rows * shards
    params = pltpu.CompilerParams(vmem_limit_bytes=VMEM_LIMIT)
    swap = [(i, i ^ 1) for i in range(shards)]

    depth = output_weight.shape[0]
    share = model // (groups * cores)
    own_w = lax.dynamic_slice_in_dim(output_weight, (group * cores + core) * share, share, 1)
    give_w = lax.dynamic_slice_in_dim(output_weight, (group * cores + 1 - core) * share, share, 1)

    cos_p, sin_p = rope_tables(me * rows + jnp.arange(rows, dtype=jnp.int32))
    table = pl.BlockSpec((rows, HD), lambda s: (0, 0))
    column = pl.BlockSpec((rows, local), lambda s: (0, s))
    kv = pl.pallas_call(
        kv_prep_kernel,
        grid=(shards,),
        in_specs=[column, column, table, table],
        out_specs=pl.BlockSpec((1, 2, rows, local), lambda s: (s, 0, 0, 0)),
        out_shape=jax.ShapeDtypeStruct((shards, 2, rows, local), jnp.bfloat16),
        compiler_params=params,
    )(prompt_key, prompt_value, cos_p, sin_p)
    kv = lax.all_to_all(kv, "seq", split_axis=0, concat_axis=0)
    q_sent = pl.pallas_call(
        q_prep_kernel,
        grid=(shards,),
        in_specs=[column, table, table],
        out_specs=pl.BlockSpec((1, rows, local), lambda s: (s, 0, 0)),
        out_shape=jax.ShapeDtypeStruct((shards, rows, local), jnp.bfloat16),
        compiler_params=params,
    )(prompt_query, cos_p, sin_p)
    q = lax.all_to_all(q_sent, "seq", split_axis=0, concat_axis=0)

    got_w = lax.ppermute(give_w, "seq", swap)
    pair_w = jnp.where(core == 0, jnp.stack([own_w, got_w]), jnp.stack([got_w, own_w]))
    same_core = [[i for i in range(shards) if i % cores == c] for c in range(cores)]
    all_w = lax.all_gather(pair_w, "seq", axis=0, tiled=True, axis_index_groups=same_core)
    all_w = all_w.reshape(width, share)

    both = jnp.concatenate(
        [response_embed, jnp.broadcast_to(mask_embed[None, :], (16, model))], axis=0
    )
    normed = rms_scale(both.astype(jnp.float32), attention_gain).astype(jnp.bfloat16)
    proj = [
        jnp.dot(normed, w, preferred_element_type=jnp.float32)
        for w in (query_weight, key_weight, value_weight)
    ]
    cos_r, sin_r = rope_tables(prompt + block_index[0] * resp + jnp.arange(resp, dtype=jnp.int32))
    commit_wide = jnp.broadcast_to(commit_step[:, None], (resp, HD))

    out_rows = resp // shards
    head_col = pl.BlockSpec((resp + 16, HD), lambda h: (0, h))
    full = pl.BlockSpec((resp, HD), lambda h: (0, 0))
    key_col = pl.BlockSpec((resp, HD), lambda h: (0, h))
    contexts, key0, value0 = pl.pallas_call(
        response_kernel,
        grid=(heads,),
        in_specs=[
            head_col, head_col, head_col,
            pl.BlockSpec((shards, 2, rows, HD), lambda h: (0, 0, 0, h)),
            full, full, full,
        ],
        out_specs=[
            pl.BlockSpec((shards, STEPS, out_rows, HD), lambda h: (0, 0, 0, h)),
            key_col, key_col,
        ],
        out_shape=[
            jax.ShapeDtypeStruct((shards, STEPS, out_rows, local), jnp.bfloat16),
            jax.ShapeDtypeStruct((resp, local), jnp.bfloat16),
            jax.ShapeDtypeStruct((resp, local), jnp.bfloat16),
        ],
        scratch_shapes=[
            pltpu.VMEM((2 * resp, HD), jnp.float32),
            pltpu.VMEM((2 * resp, HD), jnp.float32),
            pltpu.VMEM((2 * resp, HD), jnp.float32),
            pltpu.VMEM((prompt, 2 * HD), jnp.bfloat16),
            pltpu.VMEM((resp, 2 * HD), jnp.bfloat16),
            pltpu.VMEM((2 * resp, 2 * HD), jnp.float32),
            pltpu.VMEM((2 * resp, HD), jnp.float32),
        ],
        compiler_params=params,
        cost_estimate=pl.CostEstimate(
            flops=4 * heads * HD * (2 * resp * prompt * 2 + STEPS * resp * resp),
            bytes_accessed=4 * prompt * local,
            transcendentals=heads * (2 * resp * prompt + STEPS * resp * resp),
        ),
    )(*proj, kv, cos_r, sin_r, commit_wide)

    got = lax.all_to_all(contexts, "seq", split_axis=0, concat_axis=0)
    my_rows = STEPS * out_rows
    ctx = jnp.transpose(got.reshape(shards, my_rows, local), (1, 0, 2)).reshape(my_rows, width)

    q_shards = max(1, math.gcd(shards, QBLOCK // rows))
    col_h = pl.BlockSpec((resp, HD), lambda h, i: (0, h))
    prompt_local = pl.pallas_call(
        prompt_kernel,
        grid=(heads, shards // q_shards),
        in_specs=[
            pl.BlockSpec((q_shards, rows, HD), lambda h, i: (i, 0, h)),
            pl.BlockSpec((shards, 2, rows, HD), lambda h, i: (0, 0, 0, h)),
            col_h, col_h,
        ],
        out_specs=pl.BlockSpec((q_shards, rows, HD), lambda h, i: (i, 0, h)),
        out_shape=jax.ShapeDtypeStruct((shards, rows, local), jnp.bfloat16),
        scratch_shapes=[pltpu.VMEM((prompt + resp, 2 * HD), jnp.bfloat16)],
        compiler_params=params,
        cost_estimate=pl.CostEstimate(
            flops=8 * heads * HD * prompt * (prompt + resp),
            bytes_accessed=8 * prompt * local,
            transcendentals=heads * prompt * (prompt + resp),
        ),
    )(q, kv, key0, value0)
    back = lax.all_to_all(prompt_local, "seq", split_axis=0, concat_axis=0)
    prompt_context = jnp.transpose(back, (1, 0, 2)).reshape(rows, width)

    def turn(x, by):
        return lax.ppermute(x, "groups", [(g, (g + by) % groups) for g in range(groups)])

    def project(x):
        return jnp.dot(x, all_w, preferred_element_type=jnp.float32).astype(jnp.bfloat16)

    mine, sib = [], []
    for by in range(groups):
        there = ctx if by == 0 else turn(ctx, by)
        beside = lax.ppermute(there, "seq", swap)
        out = project(jnp.concatenate([there, beside], axis=0))
        home = out if by == 0 else turn(out, groups - by)
        mine.append(home[:my_rows])
        sib.append(home[my_rows:])
    own_cols = jnp.stack(mine)
    other_cols = lax.ppermute(jnp.stack(sib), "seq", swap)
    pair = jnp.where(
        core == 0, jnp.stack([own_cols, other_cols], 2), jnp.stack([other_cols, own_cols], 2)
    )
    pair = lax.dynamic_slice_in_dim(
        jnp.concatenate([pair, pair], axis=0), lax.rem(groups - group, groups), groups, 0
    )
    attn = jnp.transpose(pair, (1, 0, 2, 3)).reshape(STEPS, out_rows, model).astype(jnp.float32)

    start = me * out_rows
    my_embed = lax.dynamic_slice_in_dim(response_embed, start, out_rows, 0)
    my_commit = lax.dynamic_slice_in_dim(commit_step, start, out_rows, 0)
    shown = my_commit[None, :, None] <= jnp.arange(STEPS)[:, None, None]
    inputs = jnp.where(shown, my_embed[None], mask_embed[None, None, :]).astype(jnp.float32)
    hidden = inputs + attn
    return (
        prompt_context,
        hidden.astype(jnp.bfloat16),
        rms_scale(hidden, residual_gain).astype(jnp.bfloat16),
    )


def solution(mesh):
    return jax.shard_map(
        per_device,
        mesh=mesh,
        in_specs=(
            P(("groups", "seq"), None),
            P(("groups", "seq"), None),
            P(("groups", "seq"), None),
            P("groups", None),
            P(),
            P("groups"),
            P("groups"),
            P(),
            P(),
            P(None, "seq"),
            P(None, "seq"),
            P(None, "seq"),
            P("seq", None),
        ),
        out_specs=(
            P(("groups", "seq"), None),
            P(None, ("groups", "seq"), None),
            P(None, ("groups", "seq"), None),
        ),
        check_vma=False,
    )
```

profile of v0, /device:TPU:1, one launch (start us, length us, event | category | flops | bytes accessed | tf_op | source)
XLA Modules:
  0.0 304.3 jit_solution(13846824241622491303)
XLA Ops:
  7.2 0.0 copy-start
  7.2 0.0 all-gather.2.cloned.1.call-start
  7.3 2.4 dynamic-slice_bitcast_fusion
  9.7 0.1 collective-permute-start.1
  9.7 2.2 collective-permute-done.1
  11.9 2.7 maximum_select_fusion
  14.6 0.0 all-gather.2.cloned.1.call-update
  14.7 0.3 fusion.20
  15.0 0.1 pad_maximum_fusion.4
  15.1 0.0 copy-start.5
  15.1 1.2 copy-done.5
  16.4 2.0 shard_map.149
  18.4 1.3 copy-done.2
  19.7 7.5 %all-to-all-start.1 = ((bf16[16,2,128,256]{3,2,1,0:T(8,128)(2,1)}), bf16[16,2,128,256]{3,2,1,0:T(8,128)(2,1)}, u32[]{:S(2)}, u32[]{:S(2)}) async-start(bf16[16,2,128,256]{3,2,1,0:T(8,128)(2,1)} %copy-done.2), calls=%async_computation.1 | async-start | bytes 4194304 | tf_op jit(solution)/shard_map/all_to_all | solution.py:190
  27.2 0.0 copy-start.9
  28.0 1.0 fusion.19
  29.0 0.2 pad_maximum_fusion.2
  29.3 2.7 fusion
  32.0 3.0 fusion.2
  35.0 0.0 copy-start.15
  35.0 2.1 fusion.23.q_ref
  37.1 2.1 fusion.24.k_ref
  39.2 2.1 fusion.25.v_ref
  41.3 57.6 %all-to-all-done.1.kv_ref = bf16[16,2,128,256]{3,2,1,0:T(8,128)(2,1)} async-done(((bf16[16,2,128,256]{3,2,1,0:T(8,128)(2,1)}), bf16[16,2,128,256]{3,2,1,0:T(8,128)(2,1)}, u32[]{:S(2)}, u32[]{:S(2)}) %all-to-all-start.1) | async-done | bytes 2097184 | tf_op jit(solution)/shard_map/all_to_all | solution.py:190
  98.9 0.1 broadcast_in_dim.37.commit_ref
  99.0 0.0 copy-start.6
  99.0 1.0 copy-done.6
  100.1 1.0 copy-done.7
  101.1 1.0 copy-done.8
  102.2 18.8 %shard_map.150 = (bf16[16,4,32,256]{3,2,1,0:T(8,128)(2,1)}, bf16[512,256]{1,0:T(8,128)(2,1)S(1)}, bf16[512,256]{1,0:T(8,128)(2,1)S(1)}) custom-call(f32[528,256]{1,0:T(8,128)S(1)} %copy-done.6, f32[528,256]{1,0:T(8,128)S(1)} %copy-done.7, f32[528,256]{1,0:T(8,128)S(1)} %copy-done.8, bf16[16,2,128,256]{3,2,1,0:T(8,128)(2,1)} %all-to-all-done.1.kv_ref, ...), custom_call_target="tpu_custom_call" | custom-call | flops 5368709120 | bytes 2097152 | tf_op jit(solution)/shard_map/pallas_call | solution.py:222
  121.0 13.4 %all-to-all-start.3 = ((bf16[16,4,32,256]{3,2,1,0:T(8,128)(2,1)}), bf16[16,4,32,256]{3,2,1,0:T(8,128)(2,1)}, u32[]{:S(2)}, u32[]{:S(2)}) async-start(bf16[16,4,32,256]{3,2,1,0:T(8,128)(2,1)} %get-tuple-element.8), calls=%async_computation.3 | async-start | bytes 2097152 | tf_op jit(solution)/shard_map/all_to_all | solution.py:256
  134.5 6.0 %shard_map.148 = bf16[16,128,256]{2,1,0:T(8,128)(2,1)} custom-call(bf16[128,4096]{1,0:T(8,128)(2,1)S(1)} %copy-done.3, f32[128,128]{1,0:T(8,128)S(1)} %get-tuple-element.31.cos_ref, f32[128,128]{1,0:T(8,128)S(1)} %get-tuple-element.32.sin_ref), custom_call_target="tpu_custom_call" | custom-call | tf_op jit(solution)/shard_map/pallas_call | solution.py:191
  140.5 33.1 %all-to-all-done.3 = bf16[16,4,32,256]{3,2,1,0:T(8,128)(2,1)} async-done(((bf16[16,4,32,256]{3,2,1,0:T(8,128)(2,1)}), bf16[16,4,32,256]{3,2,1,0:T(8,128)(2,1)}, u32[]{:S(2)}, u32[]{:S(2)}) %all-to-all-start.3) | async-done | bytes 1048608 | tf_op jit(solution)/shard_map/all_to_all | solution.py:256
  173.6 19.1 %all-to-all-start = ((bf16[16,128,256]{2,1,0:T(8,128)(2,1)}), bf16[16,128,256]{2,1,0:T(8,128)(2,1)S(1)}, u32[]{:S(2)}, u32[]{:S(2)}) async-start(bf16[16,128,256]{2,1,0:T(8,128)(2,1)} %shard_map.148), calls=%async_computation | async-start | bytes 2097152 | tf_op jit(solution)/shard_map/all_to_all | solution.py:199
  192.7 2.3 copy.23
  195.0 1.6 collective-permute-start.2
  196.5 23.6 %collective-permute-done.2 = bf16[128,4096]{0,1:T(8,128)(2,1)} collective-permute-done((bf16[128,4096]{0,1:T(8,128)(2,1)}, bf16[128,4096]{0,1:T(8,128)(2,1)}, u32[]{:S(2)}, u32[]{:S(2)}) %collective-permute-start.2) | collective-permute-done | bytes 1048608 | tf_op jit(solution)/shard_map/ppermute | solution.py:284
  220.1 0.8 collective-permute-start.3
  220.9 29.5 %shard_map.151 = bf16[16,128,256]{2,1,0:T(8,128)(2,1)} custom-call(bf16[16,128,256]{2,1,0:T(8,128)(2,1)S(1)} %all-to-all-done.q_ref, bf16[16,2,128,256]{3,2,1,0:T(8,128)(2,1)} %all-to-all-done.1.kv_ref, bf16[512,256]{1,0:T(8,128)(2,1)S(1)} %get-tuple-element.6.key0_ref, bf16[512,256]{1,0:T(8,128)(2,1)S(1)} %get-tuple-element.7.value0_ref), custom_call_target="tpu_custom_call" | custom-call | flops 10737418240 | bytes 4194304 | tf_op jit(solution)/shard_map/pallas_call | solution.py:262
  250.4 6.2 %all-to-all-start.2 = ((bf16[16,128,256]{2,1,0:T(8,128)(2,1)}), bf16[16,128,256]{2,1,0:T(8,128)(2,1)S(1)}, u32[]{:S(2)}, u32[]{:S(2)}) async-start(bf16[16,128,256]{2,1,0:T(8,128)(2,1)} %shard_map.151), calls=%async_computation.2 | async-start | bytes 2097152 | tf_op jit(solution)/shard_map/all_to_all | solution.py:280
  256.6 0.0 all-gather.2.cloned.1.call-done
  256.6 6.5 %fusion.12 = bf16[256,1024]{1,0:T(8,128)(2,1)S(1)} fusion(bf16[4096,1024]{1,0:T(8,128)(2,1)} %bitcast.37, bf16[128,4096]{0,1:T(8,128)(2,1)} %collective-permute-done.3, bf16[128,4096]{0,1:T(8,128)(2,1)} %collective-permute-done.2), kind=kOutput, calls=%fused_computation.21 | convolution fusion | flops 2151940096 | bytes 11010048 | tf_op jit(solution)/shard_map/dot_general | solution.py:287
  263.1 1.6 collective-permute-start.4
  264.7 3.9 %fusion.15 = bf16[256,1024]{1,0:T(8,128)(2,1)S(1)} fusion(bf16[4096,1024]{1,0:T(8,128)(2,1)S(1)} %bitcast.38, bf16[128,4096]{0,1:T(8,128)(2,1)} %collective-permute-done, bf16[128,4096]{0,1:T(8,128)(2,1)} %bitcast.5), kind=kOutput, calls=%fused_computation.22 | convolution fusion | flops 2151940096 | bytes 11010048 | tf_op jit(solution)/shard_map/dot_general | solution.py:287
  268.6 0.7 slice_bitcast_fusion.3
  269.3 7.4 %collective-permute-done.4 = bf16[256,1024]{1,0:T(8,128)(2,1)S(1)} collective-permute-done((bf16[256,1024]{1,0:T(8,128)(2,1)S(1)}, bf16[256,1024]{1,0:T(8,128)(2,1)S(1)}, u32[]{:S(2)}, u32[]{:S(2)}) %collective-permute-start.4) | collective-permute-done | bytes 524320 | tf_op jit(solution)/shard_map/ppermute | solution.py:284
  276.7 0.7 slice_bitcast_fusion.2
  277.4 0.8 pad_maximum_fusion.1
  278.3 0.9 collective-permute-start.5
  279.1 1.0 constant_dynamic-slice_fusion.1
  280.1 0.1 dynamic_slice.15
  280.2 0.1 broadcast_in_dim.59
  280.3 0.8 broadcast_in_dim.62
  281.1 0.1 le.33
  281.2 0.1 le.35
  281.4 0.7 copy.22
  282.1 1.3 copy.27
  283.4 1.1 maximum_bitcast_fusion
  284.5 1.4 maximum_select_fusion.1
  285.9 1.0 multiply_reduce_fusion
  286.9 3.0 copy.24
  289.9 4.0 %reshape.105 = f32[4,32,4096]{2,1,0:T(8,128)} reshape(f32[128,2,2,1024]{3,2,1,0:T(2,128)} %copy.24) | data formatting | bytes 4194304 | tf_op jit(solution)/shard_map/convert_element_type | solution.py:305
  293.9 0.1 rsqrt.21
  294.0 3.4 %multiply_convert_fusion = (bf16[4,32,4096]{2,1,0:T(8,128)(2,1)}, bf16[4,32,4096]{2,1,0:T(8,128)(2,1)}) fusion(f32[4,32,4096]{2,1,0:T(8,128)} %reshape.105, f32[4096]{0:T(1024)S(1)} %convert_element_type.71, f32[4,32]{1,0:T(4,128)S(1)} %rsqrt.21, pred[4,32]{1,0:T(4,128)(4,1)S(1)} %iota_compare_fusion, bf16[4096]{0:T(1024)(128)(2,1)S(1)} %copy-done.10, ...), kind=kLoop, calls=%fused_computation.17 | loop fusion | flops 3670016 | bytes 4481664 | tf_op jit(solution)/shard_map/convert_element_type | solution.py:316
  (44 shorter events, 0.2 us)
Async XLA Ops:
  7.2 27.8 %copy-start = (bf16[4096,256]{1,0:T(8,128)(2,1)S(1)}, bf16[4096,256]{1,0:T(8,128)(2,1)}, u32[]{:S(2)}) copy-start(bf16[4096,256]{1,0:T(8,128)(2,1)} %param.22) | copy-start | bytes 6291460
  7.2 7.9 %copy-start.4 = (bf16[128,4096]{1,0:T(8,128)(2,1)S(1)}, bf16[128,4096]{1,0:T(8,128)(2,1)}, u32[]{:S(2)}) copy-start(bf16[128,4096]{1,0:T(8,128)(2,1)} %key_ref.1) | copy-start | bytes 3145732
  7.2 249.4 %all-gather.2.cloned.1.call-start = ((), (), s32[]{:S(2)}) async-start(), calls=%async_computation.4 | async-start | bytes 9437184 | tf_op jit(solution)/shard_map/all_gather | solution.py:204
  9.7 2.3 collective-permute-start.1
  15.1 1.2 copy-start.5
  16.4 10.8 %copy-start.11 = (bf16[4096]{0:T(1024)(128)(2,1)S(1)}, bf16[4096]{0:T(1024)(128)(2,1)}, u32[]{:S(2)}) copy-start(bf16[4096]{0:T(1024)(128)(2,1)} %param.20) | copy-start | bytes 24580
  18.3 1.4 copy-start.2
  19.7 9.5 %copy-start.10 = (bf16[4096]{0:T(1024)(128)(2,1)S(1)}, bf16[4096]{0:T(1024)(128)(2,1)}, u32[]{:S(2)}) copy-start(bf16[4096]{0:T(1024)(128)(2,1)} %param.17) | copy-start | bytes 24580
  19.7 79.2 %all-to-all-start.1 = ((bf16[16,2,128,256]{3,2,1,0:T(8,128)(2,1)}), bf16[16,2,128,256]{3,2,1,0:T(8,128)(2,1)}, u32[]{:S(2)}, u32[]{:S(2)}) async-start(bf16[16,2,128,256]{3,2,1,0:T(8,128)(2,1)} %copy-done.2), calls=%async_computation.1 | async-start | bytes 4194304 | tf_op jit(solution)/shard_map/all_to_all | solution.py:190
  27.2 4.8 %copy-start.9 = (bf16[512,4096]{1,0:T(8,128)(2,1)S(1)}, bf16[512,4096]{1,0:T(8,128)(2,1)}, u32[]{:S(2)}) copy-start(bf16[512,4096]{1,0:T(8,128)(2,1)} %param.16) | copy-start | bytes 12582916
  35.0 2.1 copy-start.15
  37.1 2.1 copy-start.16
  39.2 59.7 %copy-start.13 = (s32[512]{0:T(512)S(1)}, s32[512]{0:T(512)}, u32[]{:S(2)}) copy-start(s32[512]{0:T(512)} %param.18) | copy-start | bytes 6148
  99.0 1.1 copy-start.6
  100.1 1.0 copy-start.7
  101.1 1.0 copy-start.8
  102.2 32.3 %copy-start.3 = (bf16[128,4096]{1,0:T(8,128)(2,1)S(1)}, bf16[128,4096]{1,0:T(8,128)(2,1)}, u32[]{:S(2)}) copy-start(bf16[128,4096]{1,0:T(8,128)(2,1)} %query_ref.1) | copy-start | bytes 3145732
  121.0 52.6 %all-to-all-start.3 = ((bf16[16,4,32,256]{3,2,1,0:T(8,128)(2,1)}), bf16[16,4,32,256]{3,2,1,0:T(8,128)(2,1)}, u32[]{:S(2)}, u32[]{:S(2)}) async-start(bf16[16,4,32,256]{3,2,1,0:T(8,128)(2,1)} %get-tuple-element.8), calls=%async_computation.3 | async-start | bytes 2097152 | tf_op jit(solution)/shard_map/all_to_all | solution.py:256
  173.6 47.4 %all-to-all-start = ((bf16[16,128,256]{2,1,0:T(8,128)(2,1)}), bf16[16,128,256]{2,1,0:T(8,128)(2,1)S(1)}, u32[]{:S(2)}, u32[]{:S(2)}) async-start(bf16[16,128,256]{2,1,0:T(8,128)(2,1)} %shard_map.148), calls=%async_computation | async-start | bytes 2097152 | tf_op jit(solution)/shard_map/all_to_all | solution.py:199
  195.0 25.1 %collective-permute-start.2 = (bf16[128,4096]{0,1:T(8,128)(2,1)}, bf16[128,4096]{0,1:T(8,128)(2,1)}, u32[]{:S(2)}, u32[]{:S(2)}) collective-permute-start(bf16[128,4096]{0,1:T(8,128)(2,1)} %bitcast.5), channel_id=1, source_target_pairs={{0,16},{16,0},{1,17},{17,1},{2,18},{18,2},{3,19},{19,3},{4,20},{20... | collective-permute-start | bytes 3145736 | tf_op jit(solution)/shard_map/ppermute | solution.py:284
  220.1 36.5 %collective-permute-start.3 = (bf16[128,4096]{0,1:T(8,128)(2,1)}, bf16[128,4096]{0,1:T(8,128)(2,1)}, u32[]{:S(2)}, u32[]{:S(2)}) collective-permute-start(bf16[128,4096]{0,1:T(8,128)(2,1)} %collective-permute-done.2), channel_id=1, source_target_pairs={{0,1},{1,0},{2,3},{3,2},{4,5},{5,4},{6,7},{7,6},{8,9},{9,8},{10,11... | collective-permute-start | bytes 3145736 | tf_op jit(solution)/shard_map/ppermute | solution.py:292
  220.9 43.7 %collective-permute-start = (bf16[128,4096]{0,1:T(8,128)(2,1)}, bf16[128,4096]{0,1:T(8,128)(2,1)}, u32[]{:S(2)}, u32[]{:S(2)}) collective-permute-start(bf16[128,4096]{0,1:T(8,128)(2,1)} %bitcast.5), channel_id=1, source_target_pairs={{0,1},{1,0},{2,3},{3,2},{4,5},{5,4},{6,7},{7,6},{8,9},{9,8},{10,11... | collective-permute-start | bytes 3145736 | tf_op jit(solution)/shard_map/ppermute | solution.py:292
  250.4 31.0 %all-to-all-start.2 = ((bf16[16,128,256]{2,1,0:T(8,128)(2,1)}), bf16[16,128,256]{2,1,0:T(8,128)(2,1)S(1)}, u32[]{:S(2)}, u32[]{:S(2)}) async-start(bf16[16,128,256]{2,1,0:T(8,128)(2,1)} %shard_map.151), calls=%async_computation.2 | async-start | bytes 2097152 | tf_op jit(solution)/shard_map/all_to_all | solution.py:280
  256.6 8.1 %copy-start.14 = (bf16[16,256,1024]{2,1,0:T(8,128)(2,1)S(1)}, bf16[16,256,1024]{2,1,0:T(8,128)(2,1)}, u32[]{:S(2)}) copy-start(bf16[16,256,1024]{2,1,0:T(8,128)(2,1)} %all-gather.2.cloned.1.call-done) | copy-start | bytes 25165828
  263.1 13.6 %collective-permute-start.4 = (bf16[256,1024]{1,0:T(8,128)(2,1)S(1)}, bf16[256,1024]{1,0:T(8,128)(2,1)S(1)}, u32[]{:S(2)}, u32[]{:S(2)}) collective-permute-start(bf16[256,1024]{1,0:T(8,128)(2,1)S(1)} %fusion.12), channel_id=1, source_target_pairs={{0,16},{16,0},{1,17},{17,1},{2,18},{18,2},{3,19},{19,3},{4,20},{20... | collective-permute-start | bytes 1572872 | tf_op jit(solution)/shard_map/ppermute | solution.py:284
  268.6 12.7 %copy-start.12 = (bf16[4096]{0:T(1024)(128)(2,1)S(1)}, bf16[4096]{0:T(1024)(128)(2,1)}, u32[]{:S(2)}) copy-start(bf16[4096]{0:T(1024)(128)(2,1)} %param.21) | copy-start | bytes 24580
  278.3 6.2 %collective-permute-start.5 = (bf16[2,128,1024]{2,1,0:T(8,128)(2,1)}, bf16[2,128,1024]{2,1,0:T(8,128)(2,1)}, u32[]{:S(2)}, u32[]{:S(2)}) collective-permute-start(bf16[2,128,1024]{2,1,0:T(8,128)(2,1)} %pad_maximum_fusion.1), channel_id=1, source_target_pairs={{0,1},{1,0},{2,3},{3,2},{4,5},{5,4},{6,7},{7,6},{8,9},{9,8},{10,11... | collective-permute-start | bytes 1572872 | tf_op jit(solution)/shard_map/ppermute | solution.py:298
  286.9 10.5 %copy-start.1 = (bf16[4096,256]{1,0:T(8,128)(2,1)S(1)}, bf16[4096,256]{1,0:T(8,128)(2,1)}, u32[]{:S(2)}) copy-start(bf16[4096,256]{1,0:T(8,128)(2,1)} %param.22) | copy-start | bytes 6291460
Sparse Core Ops, SparseCore 0:
  14.8 200.9 all-gather.1
where the time goes:
time: 305 us; the launch traced here: 304 us
  waiting for transfers between devices  124 us (41%)
  Pallas kernels  56.3 us (18%)
  starting transfers between devices  51.1 us (17%)
  local copies, waits for them, and re-layouts  23.3 us (8%)
  other arithmetic  17.9 us (6%)
  matrix products  16.7 us (5%)
  between operations  15.2 us (5%)
    all_to_all x1, waiting for transfers between devices, per_device(): kv = lax.all_to_all(kv, 'seq', split_axis=0, concat_axis=0)  57.6 us
    all_to_all x1, waiting for transfers between devices, per_device(): got = lax.all_to_all(contexts, 'seq', split_axis=0, concat_axis=0)  33.1 us
    ppermute x2, waiting for transfers between devices, turn(): lax.ppermute(x, 'groups', [(g, (g + by) % groups) for g in range(groups)])  30.9 us
    pallas_call x1, Pallas kernels, per_device(): pl.pallas_call(prompt_kernel, grid=(heads, shards // q_shards), in_specs=...  29.5 us
    all_to_all x1, starting transfers between devices, per_device(): q = lax.all_to_all(q_sent, 'seq', split_axis=0, concat_axis=0)  19.1 us
    pallas_call x1, Pallas kernels, per_device(): pl.pallas_call(response_kernel, grid=(heads,), in_specs=[head_col, head_c...  18.8 us
    all_to_all x1, starting transfers between devices, per_device(): got = lax.all_to_all(contexts, 'seq', split_axis=0, concat_axis=0)  13.4 us
    dot_general x2, matrix products, project(): jnp.dot(x, all_w, preferred_element_type=jnp.float32).astype(jnp.bfloat16)  10.4 us
  transfers between devices with their start and end apart: 11, of which 5 were waited for; matrix products, arithmetic and copies ran while one was open for 11% of the time, Pallas kernels for 18%

commit v1 on v0

--- a/solution.py
+++ b/solution.py
@@ -1,4 +1,3 @@
-import functools
 import math
 
 import jax
@@ -150,6 +149,26 @@
     o = jnp.dot(p1, va[:prompt, :], preferred_element_type=jnp.float32)
     o += jnp.dot(p2, va[prompt:, :], preferred_element_type=jnp.float32)
     out_ref[...] = (o[:, :HD] / o[:, HD:]).astype(jnp.bfloat16).reshape(out_ref.shape)
+
+
+def finish_kernel(
+    at_ref, own_ref, other_ref, embed_ref, mask_ref, commit_ref, gain_ref,
+    residual_ref, normed_ref, hidden,
+):
+    groups, _, share = own_ref.shape
+    group, core = at_ref[0], at_ref[1]
+    for by in range(groups):
+        first = lax.rem(group + by, groups) * 2
+        for ref, c in ((own_ref, core), (other_ref, 1 - core)):
+            at = pl.ds(pl.multiple_of((first + c) * share, share), share)
+            hidden[:, at] = ref[by].astype(jnp.float32)
+    shown = commit_ref[:, :1] <= pl.program_id(0)
+    inputs = jnp.where(
+        shown, embed_ref[...].astype(jnp.float32), mask_ref[...].astype(jnp.float32)
+    )
+    h = inputs + hidden[...]
+    residual_ref[0] = h.astype(jnp.bfloat16)
+    normed_ref[0] = rms_scale(h, gain_ref[...]).astype(jnp.bfloat16)
 
 
 def per_device(
@@ -200,9 +219,11 @@
 
     got_w = lax.ppermute(give_w, "seq", swap)
     pair_w = jnp.where(core == 0, jnp.stack([own_w, got_w]), jnp.stack([got_w, own_w]))
-    same_core = [[i for i in range(shards) if i % cores == c] for c in range(cores)]
-    all_w = lax.all_gather(pair_w, "seq", axis=0, tiled=True, axis_index_groups=same_core)
-    all_w = all_w.reshape(width, share)
+    quad = 2 * cores
+    lines = [[i for i in range(shards) if i % quad == c] for c in range(quad)]
+    line_w = lax.all_gather(pair_w, "seq", axis=0, tiled=True, axis_index_groups=lines)
+    line_w = line_w.reshape(width // 2, share)
+    beside_w = lax.ppermute(line_w, "seq", [(i, i ^ cores) for i in range(shards)])
 
     both = jnp.concatenate(
         [response_embed, jnp.broadcast_to(mask_embed[None, :], (16, model))], axis=0
@@ -253,9 +274,18 @@
         ),
     )(*proj, kv, cos_r, sin_r, commit_wide)
 
+    contexts, q = lax.optimization_barrier((contexts, q))
     got = lax.all_to_all(contexts, "seq", split_axis=0, concat_axis=0)
     my_rows = STEPS * out_rows
-    ctx = jnp.transpose(got.reshape(shards, my_rows, local), (1, 0, 2)).reshape(my_rows, width)
+    pair_side = lax.rem(lax.div(me, cores), 2)
+    got = got.reshape(shards // quad, 2, cores, my_rows, local)
+    got = jnp.stack(
+        [
+            lax.dynamic_index_in_dim(got, pair_side, 1, keepdims=False),
+            lax.dynamic_index_in_dim(got, 1 - pair_side, 1, keepdims=False),
+        ]
+    )
+    ctx = jnp.transpose(got, (3, 0, 1, 2, 4)).reshape(my_rows, width)
 
     q_shards = max(1, math.gcd(shards, QBLOCK // rows))
     col_h = pl.BlockSpec((resp, HD), lambda h, i: (0, h))
@@ -284,7 +314,9 @@
         return lax.ppermute(x, "groups", [(g, (g + by) % groups) for g in range(groups)])
 
     def project(x):
-        return jnp.dot(x, all_w, preferred_element_type=jnp.float32).astype(jnp.bfloat16)
+        near = jnp.dot(x[:, : width // 2], line_w, preferred_element_type=jnp.float32)
+        far = jnp.dot(x[:, width // 2 :], beside_w, preferred_element_type=jnp.float32)
+        return (near + far).astype(jnp.bfloat16)
 
     mine, sib = [], []
     for by in range(groups):
@@ -296,25 +328,35 @@
         sib.append(home[my_rows:])
     own_cols = jnp.stack(mine)
     other_cols = lax.ppermute(jnp.stack(sib), "seq", swap)
-    pair = jnp.where(
-        core == 0, jnp.stack([own_cols, other_cols], 2), jnp.stack([other_cols, own_cols], 2)
-    )
-    pair = lax.dynamic_slice_in_dim(
-        jnp.concatenate([pair, pair], axis=0), lax.rem(groups - group, groups), groups, 0
-    )
-    attn = jnp.transpose(pair, (1, 0, 2, 3)).reshape(STEPS, out_rows, model).astype(jnp.float32)
-
     start = me * out_rows
     my_embed = lax.dynamic_slice_in_dim(response_embed, start, out_rows, 0)
-    my_commit = lax.dynamic_slice_in_dim(commit_step, start, out_rows, 0)
-    shown = my_commit[None, :, None] <= jnp.arange(STEPS)[:, None, None]
-    inputs = jnp.where(shown, my_embed[None], mask_embed[None, None, :]).astype(jnp.float32)
-    hidden = inputs + attn
-    return (
-        prompt_context,
-        hidden.astype(jnp.bfloat16),
-        rms_scale(hidden, residual_gain).astype(jnp.bfloat16),
-    )
+    my_commit = lax.dynamic_slice_in_dim(commit_wide, start, out_rows, 0)
+    part = pl.BlockSpec((groups, out_rows, share), lambda t, at: (0, t, 0))
+    row = pl.BlockSpec((1, model), lambda t, at: (0, 0))
+    result = pl.BlockSpec((1, out_rows, model), lambda t, at: (t, 0, 0))
+    out_type = jax.ShapeDtypeStruct((STEPS, out_rows, model), jnp.bfloat16)
+    residual, normed_rows = pl.pallas_call(
+        finish_kernel,
+        grid_spec=pltpu.PrefetchScalarGridSpec(
+            num_scalar_prefetch=1,
+            grid=(STEPS,),
+            in_specs=[
+                part, part,
+                pl.BlockSpec((out_rows, model), lambda t, at: (0, 0)),
+                row,
+                pl.BlockSpec((out_rows, HD), lambda t, at: (0, 0)),
+                row,
+            ],
+            out_specs=[result, result],
+            scratch_shapes=[pltpu.VMEM((out_rows, model), jnp.float32)],
+        ),
+        out_shape=[out_type, out_type],
+        compiler_params=params,
+    )(
+        jnp.stack([group, core]).astype(jnp.int32),
+        own_cols, other_cols, my_embed, mask_embed[None, :], my_commit, residual_gain[None, :],
+    )
+    return prompt_context, residual, normed_rows
 
 
 def solution(mesh):

time: 305 us -> 310 us (1.016)
  waiting for transfers between devices: 124 us -> 103 us
  starting transfers between devices: 51.1 us -> 70.3 us
  local copies, waits for them, and re-layouts: 23.3 us -> 26.7 us
    all_to_all x1, waiting for transfers between devices: 57.6 us -> 37.2 us  [per_device(): kv = lax.all_to_all(kv, 'seq', split_axis=0, concat_axis=0)]
    all_to_all x1, starting transfers between devices: 19.1 us -> 37 us  [per_device(): q = lax.all_to_all(q_sent, 'seq', split_axis=0, concat_axis=0)]
    all_to_all x1, waiting for transfers between devices: 33.1 us -> 21.8 us  [per_device(): got = lax.all_to_all(contexts, 'seq', split_axis=0, concat_axis=0)]
    ppermute x0 -> x1, waiting for transfers between devices: none -> 9.08 us  [per_device(): lax.ppermute(line_w, 'seq', [(i, i ^ cores) for i in range(shards)])]
    convert_element_type x2 -> x0, local copies, waits for them, and re-layouts: 7 us -> none  [per_device(): jnp.transpose(pair, (1, 0, 2, 3)).reshape(STEPS, out_rows, model)]
    dynamic_slice x1 -> x4, local copies, waits for them, and re-layouts: 0.08 us -> 6.42 us  [the longest x2 4.31 us: per_device(): lax.dynamic_index_in_dim(got, pair_side, 1, keepdims=False)]
    all_to_all x1, waiting for transfers between devices: 0.01 us -> 5.19 us  [per_device(): q = lax.all_to_all(q_sent, 'seq', split_axis=0, concat_axis=0)]
    unnamed x35 -> x40, local copies, waits for them, and re-layouts: 7.08 us -> 11.6 us
  transfers between devices with their start and end apart: 11 -> 12, of which waited for: 5 -> 7; matrix products, arithmetic and copies ran while one was open for 11% -> 17% of each run, Pallas kernels for 18% -> 17%
where the time goes in v1:
time: 310 us; the launch traced here: 309 us
  waiting for transfers between devices  103 us (33%)
  starting transfers between devices  70.3 us (23%)
  Pallas kernels  58 us (19%)
  local copies, waits for them, and re-layouts  26.7 us (9%)
  other arithmetic  18.2 us (6%)
  matrix products  16.9 us (5%)
  between operations  15.2 us (5%)
    all_to_all x1, waiting for transfers between devices, per_device(): kv = lax.all_to_all(kv, 'seq', split_axis=0, concat_axis=0)  37.2 us
    all_to_all x1, starting transfers between devices, per_device(): q = lax.all_to_all(q_sent, 'seq', split_axis=0, concat_axis=0)  37 us
    pallas_call x1, Pallas kernels, per_device(): pl.pallas_call(prompt_kernel, grid=(heads, shards // q_shards), in_specs=...  28.9 us
    ppermute x2, waiting for transfers between devices, turn(): lax.ppermute(x, 'groups', [(g, (g + by) % groups) for g in range(groups)])  28 us
    all_to_all x1, waiting for transfers between devices, per_device(): got = lax.all_to_all(contexts, 'seq', split_axis=0, concat_axis=0)  21.8 us
    pallas_call x1, Pallas kernels, per_device(): pl.pallas_call(response_kernel, grid=(heads,), in_specs=[head_col, head_c...  18.2 us
    all_to_all x1, starting transfers between devices, per_device(): got = lax.all_to_all(contexts, 'seq', split_axis=0, concat_axis=0)  11.8 us
    unnamed x40, local copies, waits for them, and re-layouts  11.6 us
  transfers between devices with their start and end apart: 12, of which 7 were waited for; matrix products, arithmetic and copies ran while one was open for 17% of the time, Pallas kernels for 17%

profile of v1, /device:TPU:1, one launch (start us, length us, event | category | flops | bytes accessed | tf_op | source)
XLA Modules:
  0.0 308.6 jit_solution(15150171690345684958)
XLA Ops:
  7.2 0.3 fusion.13
  7.5 0.1 pad_maximum_fusion.8
  7.6 1.4 copy-done.5
  9.0 1.2 copy-done.6
  10.3 2.0 shard_map.148
  12.2 1.4 copy-done.1
  13.7 7.5 %all-to-all-start = ((bf16[16,2,128,256]{3,2,1,0:T(8,128)(2,1)}), bf16[16,2,128,256]{3,2,1,0:T(8,128)(2,1)}, u32[]{:S(2)}, u32[]{:S(2)}) async-start(bf16[16,2,128,256]{3,2,1,0:T(8,128)(2,1)} %copy-done.1), calls=%async_computation | async-start | bytes 4194304 | tf_op jit(solution)/shard_map/all_to_all | solution.py:209
  21.1 0.0 all-gather.2.cloned.1.call-start
  21.2 2.2 dynamic-slice_bitcast_fusion
  23.5 0.2 collective-permute-start.1
  23.6 2.1 collective-permute-done.1
  25.7 2.7 maximum_select_fusion
  29.3 6.0 %shard_map.150 = bf16[16,128,256]{2,1,0:T(8,128)(2,1)} custom-call(bf16[128,4096]{1,0:T(8,128)(2,1)S(1)} %copy-done.2, f32[128,128]{1,0:T(8,128)S(1)} %get-tuple-element.37.cos_ref, f32[128,128]{1,0:T(8,128)S(1)} %get-tuple-element.38.sin_ref), custom_call_target="tpu_custom_call" | custom-call | tf_op jit(solution)/shard_map/pallas_call | solution.py:210
  35.3 3.1 %fusion = f32[528]{0:T(1024)S(1)} fusion(bf16[16,4096]{1,0:T(8,128)(2,1)S(1)} %broadcast_in_dim.10, bf16[512,4096]{1,0:T(8,128)(2,1)} %param.16), kind=kLoop, calls=%fused_computation.2 | loop fusion | flops 12975600 | bytes 4327488 | tf_op jit(solution)/shard_map/reduce_sum | solution.py:32
  38.5 1.8 fusion.12
  40.3 4.3 %fusion.2 = bf16[528,4096]{1,0:T(8,128)(2,1)} fusion(f32[4096]{0:T(1024)S(1)} %convert_element_type.30, f32[528]{0:T(1024)S(1)} %add_rsqrt_fusion, bf16[16,4096]{1,0:T(8,128)(2,1)S(1)} %broadcast_in_dim.10, bf16[512,4096]{1,0:T(8,128)(2,1)S(1)} %copy-done.9), kind=kLoop, calls=%fused_computation.4 | loop fusion | flops 15138816 | bytes 8669248 | tf_op jit(solution)/shard_map/convert_element_type | solution.py:231
  44.6 37.2 %all-to-all-done.kv_ref = bf16[16,2,128,256]{3,2,1,0:T(8,128)(2,1)} async-done(((bf16[16,2,128,256]{3,2,1,0:T(8,128)(2,1)}), bf16[16,2,128,256]{3,2,1,0:T(8,128)(2,1)}, u32[]{:S(2)}, u32[]{:S(2)}) %all-to-all-start) | async-done | bytes 2097184 | tf_op jit(solution)/shard_map/all_to_all | solution.py:209
  81.8 37.0 %all-to-all-start.1 = ((bf16[16,128,256]{2,1,0:T(8,128)(2,1)}), bf16[16,128,256]{2,1,0:T(8,128)(2,1)S(1)}, u32[]{:S(2)}, u32[]{:S(2)}) async-start(bf16[16,128,256]{2,1,0:T(8,128)(2,1)} %shard_map.150), calls=%async_computation.1 | async-start | bytes 2097152 | tf_op jit(solution)/shard_map/all_to_all | solution.py:218
  118.8 1.5 pad_maximum_fusion.6
  120.3 3.7 %fusion.16.q_ref = f32[528,256]{1,0:T(8,128)S(1)} fusion(bf16[528,4096]{1,0:T(8,128)(2,1)} %fusion.2, bf16[4096,256]{1,0:T(8,128)(2,1)S(1)} %copy-done), kind=kOutput, calls=%fused_computation.51 | convolution fusion | flops 1107296256 | bytes 6963200 | tf_op jit(solution)/shard_map/dot_general | solution.py:233
  124.0 1.3 fusion.17.k_ref
  125.3 0.3 copy-done.16
  125.6 1.3 fusion.18.v_ref
  126.9 0.1 broadcast_in_dim.11.commit_ref
  127.0 18.2 %shard_map.149 = (bf16[16,4,32,256]{3,2,1,0:T(8,128)(2,1)S(1)}, bf16[512,256]{1,0:T(8,128)(2,1)S(1)}, bf16[512,256]{1,0:T(8,128)(2,1)S(1)}) custom-call(f32[528,256]{1,0:T(8,128)S(1)} %fusion.16.q_ref, f32[528,256]{1,0:T(8,128)S(1)} %fusion.17.k_ref, f32[528,256]{1,0:T(8,128)S(1)} %fusion.18.v_ref, bf16[16,2,128,256]{3,2,1,0:T(8,128)(2,1)} %all-to-all-done.kv_ref, ...), custom_call_target="tpu_custom_call" | custom-call | flops 5368709120 | bytes 2097152 | tf_op jit(solution)/shard_map/pallas_call | solution.py:243
  145.2 1.0 copy-done.4
  146.2 0.7 copy-done.7
  146.9 5.2 %all-to-all-done.1.q_ref = bf16[16,128,256]{2,1,0:T(8,128)(2,1)S(1)} async-done(((bf16[16,128,256]{2,1,0:T(8,128)(2,1)}), bf16[16,128,256]{2,1,0:T(8,128)(2,1)S(1)}, u32[]{:S(2)}, u32[]{:S(2)}) %all-to-all-start.1) | async-done | bytes 1048608 | tf_op jit(solution)/shard_map/all_to_all | solution.py:218
  152.1 11.8 %all-to-all-start.3 = ((bf16[16,4,32,256]{3,2,1,0:T(8,128)(2,1)}), bf16[16,4,32,256]{3,2,1,0:T(8,128)(2,1)}, u32[]{:S(2)}, u32[]{:S(2)}) async-start(bf16[16,4,32,256]{3,2,1,0:T(8,128)(2,1)} %copy-done.4), calls=%async_computation.3 | async-start | bytes 2097152 | tf_op jit(solution)/shard_map/all_to_all | solution.py:278
  163.9 1.5 collective-permute-start.2
  165.3 21.8 %all-to-all-done.3 = bf16[16,4,32,256]{3,2,1,0:T(8,128)(2,1)} async-done(((bf16[16,4,32,256]{3,2,1,0:T(8,128)(2,1)}), bf16[16,4,32,256]{3,2,1,0:T(8,128)(2,1)}, u32[]{:S(2)}, u32[]{:S(2)}) %all-to-all-start.3) | async-done | bytes 1048608 | tf_op jit(solution)/shard_map/all_to_all | solution.py:278
  187.1 2.3 constant_dynamic-slice_fusion.3
  189.4 2.0 copy.22
  191.4 2.0 copy.21
  193.5 2.3 pad_maximum_fusion.3
  195.7 0.4 collective-permute-start.3
  196.1 0.1 dynamic_slice.24
  196.2 0.1 pad_add_fusion.at_ref
  196.3 24.6 %collective-permute-done.3 = bf16[128,4096]{0,1:T(8,128)(2,1)} collective-permute-done((bf16[128,4096]{0,1:T(8,128)(2,1)}, bf16[128,4096]{0,1:T(8,128)(2,1)}, u32[]{:S(2)}, u32[]{:S(2)}) %collective-permute-start.3) | collective-permute-done | bytes 1048608 | tf_op jit(solution)/shard_map/ppermute | solution.py:314
  220.9 0.7 collective-permute-start.4
  221.6 0.9 copy-done.8
  222.6 28.9 %shard_map.151 = bf16[16,128,256]{2,1,0:T(8,128)(2,1)S(1)} custom-call(bf16[16,128,256]{2,1,0:T(8,128)(2,1)S(1)} %all-to-all-done.1.q_ref, bf16[16,2,128,256]{3,2,1,0:T(8,128)(2,1)} %all-to-all-done.kv_ref, bf16[512,256]{1,0:T(8,128)(2,1)S(1)} %get-tuple-element.12.key0_ref, bf16[512,256]{1,0:T(8,128)(2,1)S(1)} %copy-done.8), custom_call_target="tpu_custom_call" | custom-call | flops 10737418240 | bytes 4194304 | tf_op jit(solution)/shard_map/pallas_call | solution.py:292
  251.5 1.0 copy-done.3
  252.5 6.7 %all-to-all-start.2 = ((bf16[16,128,256]{2,1,0:T(8,128)(2,1)}), bf16[16,128,256]{2,1,0:T(8,128)(2,1)}, u32[]{:S(2)}, u32[]{:S(2)}) async-start(bf16[16,128,256]{2,1,0:T(8,128)(2,1)} %copy-done.3), calls=%async_computation.2 | async-start | bytes 2097152 | tf_op jit(solution)/shard_map/all_to_all | solution.py:310
  259.2 0.2 collective-permute-start
  259.4 1.4 constant_dynamic-update-slice_fusion.1
  260.8 1.5 constant_dynamic-update-slice_fusion
  262.3 9.1 %collective-permute-done.2 = bf16[2048,1024]{1,0:T(8,128)(2,1)} collective-permute-done((bf16[2048,1024]{1,0:T(8,128)(2,1)}, bf16[2048,1024]{1,0:T(8,128)(2,1)}, u32[]{:S(2)}, u32[]{:S(2)}) %collective-permute-start.2) | collective-permute-done | bytes 4194336 | tf_op jit(solution)/shard_map/ppermute | solution.py:226
  271.4 3.5 %fusion.7 = f32[256,1024]{1,0:T(8,128)S(1)} fusion(bf16[2048,1024]{1,0:T(8,128)(2,1)} %collective-permute-done.2, bf16[256,4096]{0,1:T(8,128)(2,1)S(1)} %constant_dynamic-update-slice_fusion), kind=kOutput, calls=%fused_computation.13 | convolution fusion | flops 1073741824 | bytes 6291456 | tf_op jit(solution)/shard_map/dot_general | solution.py:318
  274.9 1.3 fusion.4
  276.2 0.4 collective-permute-start.5
  276.6 3.6 %fusion.10 = f32[256,1024]{1,0:T(8,128)S(1)} fusion(bf16[2048,1024]{1,0:T(8,128)(2,1)} %collective-permute-done.2, bf16[128,4096]{0,1:T(8,128)(2,1)S(1)} %collective-permute-done, bf16[128,4096]{0,1:T(8,128)(2,1)} %bitcast.9), kind=kOutput, calls=%fused_computation.17 | convolution fusion | flops 1075838976 | bytes 7340032 | tf_op jit(solution)/shard_map/dot_general | solution.py:318
  280.2 2.3 fusion.3
  282.6 0.8 slice_bitcast_fusion.1
  283.3 3.3 %collective-permute-done.5 = bf16[256,1024]{1,0:T(8,128)(2,1)S(1)} collective-permute-done((bf16[256,1024]{1,0:T(8,128)(2,1)S(1)}, bf16[256,1024]{1,0:T(8,128)(2,1)S(1)}, u32[]{:S(2)}, u32[]{:S(2)}) %collective-permute-start.5) | collective-permute-done | bytes 524320 | tf_op jit(solution)/shard_map/ppermute | solution.py:314
  286.7 0.8 slice_bitcast_fusion
  287.4 0.8 pad_maximum_fusion.5
  288.3 3.9 %collective-permute-start.6 = (bf16[2,128,1024]{2,1,0:T(8,128)(2,1)}, bf16[2,128,1024]{2,1,0:T(8,128)(2,1)S(1)}, u32[]{:S(2)}, u32[]{:S(2)}) collective-permute-start(bf16[2,128,1024]{2,1,0:T(8,128)(2,1)} %pad_maximum_fusion.5), channel_id=1, source_target_pairs={{0,1},{1,0},{2,3},{3,2},{4,5},{5,4},{6,7},{7,6},{8,9},{9,8},{10,11... | collective-permute-start | bytes 1572872 | tf_op jit(solution)/shard_map/ppermute | solution.py:330
  292.2 1.0 constant_dynamic-slice_fusion.embed_ref
  293.1 2.3 copy.20
  295.4 2.3 copy.23
  297.7 1.1 pad_maximum_fusion.4.own_ref
  298.8 0.1 broadcast_in_dim.13.commit_ref
  298.8 2.9 shard_map.152
  (45 shorter events, 0.2 us)
Async XLA Ops:
  7.2 113.1 %copy-start = (bf16[4096,256]{1,0:T(8,128)(2,1)S(1)}, bf16[4096,256]{1,0:T(8,128)(2,1)}, u32[]{:S(2)}) copy-start(bf16[4096,256]{1,0:T(8,128)(2,1)} %param.22) | copy-start | bytes 6291460
  7.6 1.4 copy-start.5
  9.0 1.2 copy-start.6
  12.2 1.4 copy-start.1
  13.7 14.8 %copy-start.11 = (bf16[4096]{0:T(1024)(128)(2,1)S(1)}, bf16[4096]{0:T(1024)(128)(2,1)}, u32[]{:S(2)}) copy-start(bf16[4096]{0:T(1024)(128)(2,1)} %param.20) | copy-start | bytes 24580
  13.7 15.7 %copy-start.2 = (bf16[128,4096]{1,0:T(8,128)(2,1)S(1)}, bf16[128,4096]{1,0:T(8,128)(2,1)}, u32[]{:S(2)}) copy-start(bf16[128,4096]{1,0:T(8,128)(2,1)} %query_ref.1) | copy-start | bytes 3145732
  13.7 68.1 %all-to-all-start = ((bf16[16,2,128,256]{3,2,1,0:T(8,128)(2,1)}), bf16[16,2,128,256]{3,2,1,0:T(8,128)(2,1)}, u32[]{:S(2)}, u32[]{:S(2)}) async-start(bf16[16,2,128,256]{3,2,1,0:T(8,128)(2,1)} %copy-done.1), calls=%async_computation | async-start | bytes 4194304 | tf_op jit(solution)/shard_map/all_to_all | solution.py:209
  21.1 14.2 %copy-start.10 = (bf16[4096]{0:T(1024)(128)(2,1)S(1)}, bf16[4096]{0:T(1024)(128)(2,1)}, u32[]{:S(2)}) copy-start(bf16[4096]{0:T(1024)(128)(2,1)} %param.17) | copy-start | bytes 24580
  21.1 142.7 %all-gather.2.cloned.1.call-start = ((), (), s32[]{:S(2)}) async-start(), calls=%async_computation.4 | async-start | bytes 5242880 | tf_op jit(solution)/shard_map/all_gather | solution.py:224
  23.5 2.3 collective-permute-start.1
  28.5 11.8 %copy-start.9 = (bf16[512,4096]{1,0:T(8,128)(2,1)S(1)}, bf16[512,4096]{1,0:T(8,128)(2,1)}, u32[]{:S(2)}) copy-start(bf16[512,4096]{1,0:T(8,128)(2,1)} %param.16) | copy-start | bytes 12582916
  81.8 70.3 %all-to-all-start.1 = ((bf16[16,128,256]{2,1,0:T(8,128)(2,1)}), bf16[16,128,256]{2,1,0:T(8,128)(2,1)S(1)}, u32[]{:S(2)}, u32[]{:S(2)}) async-start(bf16[16,128,256]{2,1,0:T(8,128)(2,1)} %shard_map.150), calls=%async_computation.1 | async-start | bytes 2097152 | tf_op jit(solution)/shard_map/all_to_all | solution.py:218
  118.8 5.2 %slice-start = ((s8[4325376]{0:T(1024)(128)(4,1)}), s8[4194304]{0:T(1024)(128)(4,1)S(1)}, s32[]{:S(2)}) async-start(s8[4325376]{0:T(1024)(128)(4,1)} %bitcast.33), calls=%async_computation.5 | async-start | bytes 8388608
  120.3 3.7 %slice-start.1 = ((s8[4325376]{0:T(1024)(128)(4,1)}), s8[131072]{0:T(1024)(128)(4,1)S(1)}, s32[]{:S(2)}) async-start(s8[4325376]{0:T(1024)(128)(4,1)} %bitcast.33), calls=%async_computation.6 | async-start | bytes 262144
  120.3 3.7 %copy-start.15 = (bf16[4096,256]{1,0:T(8,128)(2,1)S(1)}, bf16[4096,256]{1,0:T(8,128)(2,1)}, u32[]{:S(2)}) copy-start(bf16[4096,256]{1,0:T(8,128)(2,1)} %param.23) | copy-start | bytes 6291460
  124.0 1.6 copy-start.16
  125.6 1.3 copy-start.13
  145.2 1.0 copy-start.4
  146.2 0.7 copy-start.7
  152.1 44.1 %copy-start.12 = (bf16[4096]{0:T(1024)(128)(2,1)S(1)}, bf16[4096]{0:T(1024)(128)(2,1)}, u32[]{:S(2)}) copy-start(bf16[4096]{0:T(1024)(128)(2,1)} %param.21) | copy-start | bytes 24580
  152.1 35.0 %all-to-all-start.3 = ((bf16[16,4,32,256]{3,2,1,0:T(8,128)(2,1)}), bf16[16,4,32,256]{3,2,1,0:T(8,128)(2,1)}, u32[]{:S(2)}, u32[]{:S(2)}) async-start(bf16[16,4,32,256]{3,2,1,0:T(8,128)(2,1)} %copy-done.4), calls=%async_computation.3 | async-start | bytes 2097152 | tf_op jit(solution)/shard_map/all_to_all | solution.py:278
  163.9 107.5 %collective-permute-start.2 = (bf16[2048,1024]{1,0:T(8,128)(2,1)}, bf16[2048,1024]{1,0:T(8,128)(2,1)}, u32[]{:S(2)}, u32[]{:S(2)}) collective-permute-start(bf16[2048,1024]{1,0:T(8,128)(2,1)} %bitcast.38), channel_id=1, source_target_pairs={{0,2},{1,3},{2,0},{3,1},{4,6},{5,7},{6,4},{7,5},{8,10},{9,11},{10,... | collective-permute-start | bytes 12582920 | tf_op jit(solution)/shard_map/ppermute | solution.py:226
  195.7 25.2 %collective-permute-start.3 = (bf16[128,4096]{0,1:T(8,128)(2,1)}, bf16[128,4096]{0,1:T(8,128)(2,1)}, u32[]{:S(2)}, u32[]{:S(2)}) collective-permute-start(bf16[128,4096]{0,1:T(8,128)(2,1)} %bitcast.9), channel_id=1, source_target_pairs={{0,16},{16,0},{1,17},{17,1},{2,18},{18,2},{3,19},{19,3},{4,20},{20... | collective-permute-start | bytes 3145736 | tf_op jit(solution)/shard_map/ppermute | solution.py:314
  220.9 39.9 %collective-permute-start.4 = (bf16[128,4096]{0,1:T(8,128)(2,1)}, bf16[128,4096]{0,1:T(8,128)(2,1)}, u32[]{:S(2)}, u32[]{:S(2)}) collective-permute-start(bf16[128,4096]{0,1:T(8,128)(2,1)} %collective-permute-done.3), channel_id=1, source_target_pairs={{0,1},{1,0},{2,3},{3,2},{4,5},{5,4},{6,7},{7,6},{8,9},{9,8},{10,11... | collective-permute-start | bytes 3145736 | tf_op jit(solution)/shard_map/ppermute | solution.py:324
  221.6 0.9 copy-start.8
  251.5 1.0 copy-start.3
  252.5 40.6 %all-to-all-start.2 = ((bf16[16,128,256]{2,1,0:T(8,128)(2,1)}), bf16[16,128,256]{2,1,0:T(8,128)(2,1)}, u32[]{:S(2)}, u32[]{:S(2)}) async-start(bf16[16,128,256]{2,1,0:T(8,128)(2,1)} %copy-done.3), calls=%async_computation.2 | async-start | bytes 2097152 | tf_op jit(solution)/shard_map/all_to_all | solution.py:310
  259.2 17.4 %collective-permute-start = (bf16[128,4096]{0,1:T(8,128)(2,1)}, bf16[128,4096]{0,1:T(8,128)(2,1)S(1)}, u32[]{:S(2)}, u32[]{:S(2)}) collective-permute-start(bf16[128,4096]{0,1:T(8,128)(2,1)} %bitcast.9), channel_id=1, source_target_pairs={{0,1},{1,0},{2,3},{3,2},{4,5},{5,4},{6,7},{7,6},{8,9},{9,8},{10,11... | collective-permute-start | bytes 3145736 | tf_op jit(solution)/shard_map/ppermute | solution.py:324
  262.3 12.6 %copy-start.14 = (bf16[8,256,1024]{2,1,0:T(8,128)(2,1)S(1)}, bf16[8,256,1024]{2,1,0:T(8,128)(2,1)}, u32[]{:S(2)}) copy-start(bf16[8,256,1024]{2,1,0:T(8,128)(2,1)} %all-gather.2.cloned.1.call-done) | copy-start | bytes 12582916
  276.2 10.5 %collective-permute-start.5 = (bf16[256,1024]{1,0:T(8,128)(2,1)S(1)}, bf16[256,1024]{1,0:T(8,128)(2,1)S(1)}, u32[]{:S(2)}, u32[]{:S(2)}) collective-permute-start(bf16[256,1024]{1,0:T(8,128)(2,1)S(1)} %fusion.4), channel_id=1, source_target_pairs={{0,16},{16,0},{1,17},{17,1},{2,18},{18,2},{3,19},{19,3},{4,20},{20... | collective-permute-start | bytes 1572872 | tf_op jit(solution)/shard_map/ppermute | solution.py:314
  288.3 10.5 %collective-permute-start.6 = (bf16[2,128,1024]{2,1,0:T(8,128)(2,1)}, bf16[2,128,1024]{2,1,0:T(8,128)(2,1)S(1)}, u32[]{:S(2)}, u32[]{:S(2)}) collective-permute-start(bf16[2,128,1024]{2,1,0:T(8,128)(2,1)} %pad_maximum_fusion.5), channel_id=1, source_target_pairs={{0,1},{1,0},{2,3},{3,2},{4,5},{5,4},{6,7},{7,6},{8,9},{9,8},{10,11... | collective-permute-start | bytes 1572872 | tf_op jit(solution)/shard_map/ppermute | solution.py:330
Sparse Core Ops, SparseCore 0:
  28.6 131.5 all-gather.1

commit v2 on v1

--- a/solution.py
+++ b/solution.py
@@ -151,17 +151,14 @@
     out_ref[...] = (o[:, :HD] / o[:, HD:]).astype(jnp.bfloat16).reshape(out_ref.shape)
 
 
-def finish_kernel(
-    at_ref, own_ref, other_ref, embed_ref, mask_ref, commit_ref, gain_ref,
-    residual_ref, normed_ref, hidden,
-):
-    groups, _, share = own_ref.shape
-    group, core = at_ref[0], at_ref[1]
-    for by in range(groups):
-        first = lax.rem(group + by, groups) * 2
-        for ref, c in ((own_ref, core), (other_ref, 1 - core)):
-            at = pl.ds(pl.multiple_of((first + c) * share, share), share)
-            hidden[:, at] = ref[by].astype(jnp.float32)
+def finish_kernel(at_ref, *refs):
+    groups = len(refs) - 7
+    pieces = refs[:groups]
+    embed_ref, mask_ref, commit_ref, gain_ref, residual_ref, normed_ref, hidden = refs[groups:]
+    share = pieces[0].shape[1]
+    for by, ref in enumerate(pieces):
+        at = lax.rem(at_ref[0] + by, groups) * share
+        hidden[:, pl.ds(pl.multiple_of(at, share), share)] = ref[...].astype(jnp.float32)
     shown = commit_ref[:, :1] <= pl.program_id(0)
     inputs = jnp.where(
         shown, embed_ref[...].astype(jnp.float32), mask_ref[...].astype(jnp.float32)
@@ -182,18 +179,14 @@
     groups = lax.axis_size("groups")
     me = lax.axis_index("seq")
     group = lax.axis_index("groups")
-    cores = 2
-    core = lax.rem(me, cores)
     local = query_weight.shape[1]
     heads = local // HD
     prompt = rows * shards
     params = pltpu.CompilerParams(vmem_limit_bytes=VMEM_LIMIT)
-    swap = [(i, i ^ 1) for i in range(shards)]
-
-    depth = output_weight.shape[0]
-    share = model // (groups * cores)
-    own_w = lax.dynamic_slice_in_dim(output_weight, (group * cores + core) * share, share, 1)
-    give_w = lax.dynamic_slice_in_dim(output_weight, (group * cores + 1 - core) * share, share, 1)
+
+    share = model // groups
+    own_w = lax.dynamic_slice_in_dim(output_weight, group * share, share, 1)
+    all_w = lax.all_gather(own_w, "seq", axis=0, tiled=True)
 
     cos_p, sin_p = rope_tables(me * rows + jnp.arange(rows, dtype=jnp.int32))
     table = pl.BlockSpec((rows, HD), lambda s: (0, 0))
@@ -216,14 +209,6 @@
         compiler_params=params,
     )(prompt_query, cos_p, sin_p)
     q = lax.all_to_all(q_sent, "seq", split_axis=0, concat_axis=0)
-
-    got_w = lax.ppermute(give_w, "seq", swap)
-    pair_w = jnp.where(core == 0, jnp.stack([own_w, got_w]), jnp.stack([got_w, own_w]))
-    quad = 2 * cores
-    lines = [[i for i in range(shards) if i % quad == c] for c in range(quad)]
-    line_w = lax.all_gather(pair_w, "seq", axis=0, tiled=True, axis_index_groups=lines)
-    line_w = line_w.reshape(width // 2, share)
-    beside_w = lax.ppermute(line_w, "seq", [(i, i ^ cores) for i in range(shards)])
 
     both = jnp.concatenate(
         [response_embed, jnp.broadcast_to(mask_embed[None, :], (16, model))], axis=0
@@ -277,15 +262,7 @@
     contexts, q = lax.optimization_barrier((contexts, q))
     got = lax.all_to_all(contexts, "seq", split_axis=0, concat_axis=0)
     my_rows = STEPS * out_rows
-    pair_side = lax.rem(lax.div(me, cores), 2)
-    got = got.reshape(shards // quad, 2, cores, my_rows, local)
-    got = jnp.stack(
-        [
-            lax.dynamic_index_in_dim(got, pair_side, 1, keepdims=False),
-            lax.dynamic_index_in_dim(got, 1 - pair_side, 1, keepdims=False),
-        ]
-    )
-    ctx = jnp.transpose(got, (3, 0, 1, 2, 4)).reshape(my_rows, width)
+    got = got.reshape(shards, my_rows, local)
 
     q_shards = max(1, math.gcd(shards, QBLOCK // rows))
     col_h = pl.BlockSpec((resp, HD), lambda h, i: (0, h))
@@ -307,31 +284,24 @@
             transcendentals=heads * prompt * (prompt + resp),
         ),
     )(q, kv, key0, value0)
+    got, prompt_local = lax.optimization_barrier((got, prompt_local))
+    ctx = jnp.transpose(got, (1, 0, 2)).reshape(my_rows, width)
     back = lax.all_to_all(prompt_local, "seq", split_axis=0, concat_axis=0)
     prompt_context = jnp.transpose(back, (1, 0, 2)).reshape(rows, width)
 
     def turn(x, by):
         return lax.ppermute(x, "groups", [(g, (g + by) % groups) for g in range(groups)])
 
-    def project(x):
-        near = jnp.dot(x[:, : width // 2], line_w, preferred_element_type=jnp.float32)
-        far = jnp.dot(x[:, width // 2 :], beside_w, preferred_element_type=jnp.float32)
-        return (near + far).astype(jnp.bfloat16)
-
-    mine, sib = [], []
+    pieces = []
     for by in range(groups):
-        there = ctx if by == 0 else turn(ctx, by)
-        beside = lax.ppermute(there, "seq", swap)
-        out = project(jnp.concatenate([there, beside], axis=0))
-        home = out if by == 0 else turn(out, groups - by)
-        mine.append(home[:my_rows])
-        sib.append(home[my_rows:])
-    own_cols = jnp.stack(mine)
-    other_cols = lax.ppermute(jnp.stack(sib), "seq", swap)
+        there = turn(ctx, by) if by else ctx
+        out = jnp.dot(there, all_w, preferred_element_type=jnp.float32).astype(jnp.bfloat16)
+        pieces.append(turn(out, groups - by) if by else out)
+
     start = me * out_rows
     my_embed = lax.dynamic_slice_in_dim(response_embed, start, out_rows, 0)
     my_commit = lax.dynamic_slice_in_dim(commit_wide, start, out_rows, 0)
-    part = pl.BlockSpec((groups, out_rows, share), lambda t, at: (0, t, 0))
+    part = pl.BlockSpec((out_rows, share), lambda t, at: (t, 0))
     row = pl.BlockSpec((1, model), lambda t, at: (0, 0))
     result = pl.BlockSpec((1, out_rows, model), lambda t, at: (t, 0, 0))
     out_type = jax.ShapeDtypeStruct((STEPS, out_rows, model), jnp.bfloat16)
@@ -341,7 +311,7 @@
             num_scalar_prefetch=1,
             grid=(STEPS,),
             in_specs=[
-                part, part,
+                *[part] * groups,
                 pl.BlockSpec((out_rows, model), lambda t, at: (0, 0)),
                 row,
                 pl.BlockSpec((out_rows, HD), lambda t, at: (0, 0)),
@@ -353,8 +323,8 @@
         out_shape=[out_type, out_type],
         compiler_params=params,
     )(
-        jnp.stack([group, core]).astype(jnp.int32),
-        own_cols, other_cols, my_embed, mask_embed[None, :], my_commit, residual_gain[None, :],
+        group[None].astype(jnp.int32),
+        *pieces, my_embed, mask_embed[None, :], my_commit, residual_gain[None, :],
     )
     return prompt_context, residual, normed_rows
 

time: 310 us -> 278 us (0.90)
  starting transfers between devices: 70.3 us -> 53.2 us
  local copies, waits for them, and re-layouts: 26.7 us -> 17.9 us
  other arithmetic: 18.2 us -> 10.7 us
  matrix products: 16.9 us -> 23.5 us
  waiting for transfers between devices: 103 us -> 98.5 us
    all_to_all x1, starting transfers between devices: 37 us -> 12.8 us  [per_device(): q = lax.all_to_all(q_sent, 'seq', split_axis=0, concat_axis=0)]
    ppermute x2, waiting for transfers between devices: 28 us -> 4.23 us  [turn(): lax.ppermute(x, 'groups', [(g, (g + by) % groups) for g in range(groups)])]
    all_to_all x1, waiting for transfers between devices: 0.01 us -> 19.2 us  [per_device(): back = lax.all_to_all(prompt_local, 'seq', split_axis=0, concat_axis=0)]
    all_to_all x1, waiting for transfers between devices: 37.2 us -> 55.3 us  [per_device(): kv = lax.all_to_all(kv, 'seq', split_axis=0, concat_axis=0)]
    all_to_all x1, waiting for transfers between devices: 21.8 us -> 8.26 us  [per_device(): got = lax.all_to_all(contexts, 'seq', split_axis=0, concat_axis=0)]
    ppermute x5 -> x0, waiting for transfers between devices: 11.2 us -> none  [the longest x1 9.08 us: per_device(): lax.ppermute(line_w, 'seq', [(i, i ^ cores) for i in range(shards)])]
    all_to_all x1, starting transfers between devices: 11.8 us -> 19.5 us  [per_device(): got = lax.all_to_all(contexts, 'seq', split_axis=0, concat_axis=0)]
    ppermute x5 -> x0, starting transfers between devices: 6.47 us -> none  [the longest x1 3.92 us: per_device(): other_cols = lax.ppermute(jnp.stack(sib), 'seq', swap)]
  transfers between devices with their start and end apart: 12 -> 7, of which waited for: 7 -> 5; matrix products, arithmetic and copies ran while one was open for 17% -> 12% of each run, Pallas kernels for 17% -> 20%
where the time goes in v2:
time: 278 us; the launch traced here: 276 us
  waiting for transfers between devices  98.5 us (35%)
  Pallas kernels  57.4 us (21%)
  starting transfers between devices  53.2 us (19%)
  matrix products  23.5 us (8%)
  local copies, waits for them, and re-layouts  17.9 us (6%)
  between operations  15.1 us (5%)
  other arithmetic  10.7 us (4%)
    all_to_all x1, waiting for transfers between devices, per_device(): kv = lax.all_to_all(kv, 'seq', split_axis=0, concat_axis=0)  55.3 us
    pallas_call x1, Pallas kernels, per_device(): pl.pallas_call(prompt_kernel, grid=(heads, shards // q_shards), in_specs=...  28.9 us
    all_to_all x1, starting transfers between devices, per_device(): got = lax.all_to_all(contexts, 'seq', split_axis=0, concat_axis=0)  19.5 us
    all_to_all x1, waiting for transfers between devices, per_device(): back = lax.all_to_all(prompt_local, 'seq', split_axis=0, concat_axis=0)  19.2 us
    pallas_call x1, Pallas kernels, per_device(): pl.pallas_call(response_kernel, grid=(heads,), in_specs=[head_col, head_c...  18.2 us
    dot_general x2, matrix products, per_device(): jnp.dot(there, all_w, preferred_element_type=jnp.float32)  16.6 us
    all_to_all x1, starting transfers between devices, per_device(): q = lax.all_to_all(q_sent, 'seq', split_axis=0, concat_axis=0)  12.8 us
    unnamed x37, local copies, waits for them, and re-layouts  11.6 us
  transfers between devices with their start and end apart: 7, of which 5 were waited for; matrix products, arithmetic and copies ran while one was open for 12% of the time, Pallas kernels for 20%

profile of v2, /device:TPU:1, one launch (start us, length us, event | category | flops | bytes accessed | tf_op | source)
XLA Modules:
  0.0 276.4 jit_solution(12514612174844497372)
XLA Ops:
  7.2 0.0 copy-start
  7.2 0.0 all-gather.2.cloned.1.call-start
  7.2 1.5 copy-done
  8.8 1.1 constant_dynamic-slice_fusion.1
  9.9 0.0 all-gather.2.cloned.1.call-update
  9.9 0.3 fusion.4
  10.2 0.0 copy-start.11
  10.2 0.1 pad_maximum_fusion.3
  10.3 0.0 copy-start.2
  10.4 0.0 copy-start.5
  10.4 1.3 copy-done.5
  11.7 1.2 copy-done.6
  12.9 2.0 shard_map.148
  14.9 0.0 copy-start.1
  14.9 1.4 copy-done.1
  16.3 7.3 %all-to-all-start = ((bf16[16,2,128,256]{3,2,1,0:T(8,128)(2,1)}), bf16[16,2,128,256]{3,2,1,0:T(8,128)(2,1)}, u32[]{:S(2)}, u32[]{:S(2)}) async-start(bf16[16,2,128,256]{3,2,1,0:T(8,128)(2,1)} %copy-done.1), calls=%async_computation | async-start | bytes 4194304 | tf_op jit(solution)/shard_map/all_to_all | solution.py:202
  23.6 0.0 copy-done.11
  23.6 0.0 copy-start.9
  24.5 0.0 copy-done.2
  24.5 6.0 %shard_map.150 = bf16[16,128,256]{2,1,0:T(8,128)(2,1)} custom-call(bf16[128,4096]{1,0:T(8,128)(2,1)S(1)} %copy-done.2, f32[128,128]{1,0:T(8,128)S(1)} %get-tuple-element.30.cos_ref, f32[128,128]{1,0:T(8,128)S(1)} %get-tuple-element.31.sin_ref), custom_call_target="tpu_custom_call" | custom-call | tf_op jit(solution)/shard_map/pallas_call | solution.py:203
  30.5 0.0 copy-done.10
  30.5 2.7 fusion
  33.2 1.8 fusion.3
  35.1 0.0 copy-done.9
  35.1 4.3 %fusion.2 = bf16[528,4096]{1,0:T(8,128)(2,1)} fusion(f32[4096]{0:T(1024)S(1)} %convert_element_type.30, f32[528]{0:T(1024)S(1)} %add_rsqrt_fusion, bf16[16,4096]{1,0:T(8,128)(2,1)S(1)} %broadcast_in_dim.12, bf16[512,4096]{1,0:T(8,128)(2,1)S(1)} %copy-done.9), kind=kLoop, calls=%fused_computation.4 | loop fusion | flops 15138816 | bytes 8669248 | tf_op jit(solution)/shard_map/convert_element_type | solution.py:216
  39.3 55.3 %all-to-all-done.kv_ref = bf16[16,2,128,256]{3,2,1,0:T(8,128)(2,1)} async-done(((bf16[16,2,128,256]{3,2,1,0:T(8,128)(2,1)}), bf16[16,2,128,256]{3,2,1,0:T(8,128)(2,1)}, u32[]{:S(2)}, u32[]{:S(2)}) %all-to-all-start) | async-done | bytes 2097184 | tf_op jit(solution)/shard_map/all_to_all | solution.py:202
  94.6 12.8 %all-to-all-start.1 = ((bf16[16,128,256]{2,1,0:T(8,128)(2,1)}), bf16[16,128,256]{2,1,0:T(8,128)(2,1)S(1)}, u32[]{:S(2)}, u32[]{:S(2)}) async-start(bf16[16,128,256]{2,1,0:T(8,128)(2,1)} %shard_map.150), calls=%async_computation.1 | async-start | bytes 2097152 | tf_op jit(solution)/shard_map/all_to_all | solution.py:211
  107.5 1.5 pad_maximum_fusion.1
  109.0 0.0 slice-start.1
  109.0 0.0 copy-start.14
  109.0 4.4 %fusion.5.q_ref = f32[528,256]{1,0:T(8,128)S(1)} fusion(bf16[528,4096]{1,0:T(8,128)(2,1)} %fusion.2, bf16[4096,256]{1,0:T(8,128)(2,1)} %param.22), kind=kOutput, calls=%fused_computation.24 | convolution fusion | flops 1107296256 | bytes 6963200 | tf_op jit(solution)/shard_map/dot_general | solution.py:218
  113.4 0.0 slice-done
  113.4 0.0 copy-start.15
  113.4 1.3 fusion.6.k_ref
  114.7 0.3 copy-done.15
  115.0 1.3 fusion.7.v_ref
  116.3 0.0 copy-done.13
  116.3 0.1 broadcast_in_dim.13.commit_ref
  116.4 18.2 %shard_map.149 = (bf16[16,4,32,256]{3,2,1,0:T(8,128)(2,1)S(1)}, bf16[512,256]{1,0:T(8,128)(2,1)S(1)}, bf16[512,256]{1,0:T(8,128)(2,1)S(1)}) custom-call(f32[528,256]{1,0:T(8,128)S(1)} %fusion.5.q_ref, f32[528,256]{1,0:T(8,128)S(1)} %fusion.6.k_ref, f32[528,256]{1,0:T(8,128)S(1)} %fusion.7.v_ref, bf16[16,2,128,256]{3,2,1,0:T(8,128)(2,1)} %all-to-all-done.kv_ref, ...), custom_call_target="tpu_custom_call" | custom-call | flops 5368709120 | bytes 2097152 | tf_op jit(solution)/shard_map/pallas_call | solution.py:228
  134.6 0.0 copy-start.4
  134.6 1.0 copy-done.4
  135.6 0.7 copy-done.7
  136.3 11.6 %all-to-all-done.1.q_ref = bf16[16,128,256]{2,1,0:T(8,128)(2,1)S(1)} async-done(((bf16[16,128,256]{2,1,0:T(8,128)(2,1)}), bf16[16,128,256]{2,1,0:T(8,128)(2,1)S(1)}, u32[]{:S(2)}, u32[]{:S(2)}) %all-to-all-start.1) | async-done | bytes 1048608 | tf_op jit(solution)/shard_map/all_to_all | solution.py:211
  147.9 19.5 %all-to-all-start.2 = ((bf16[16,4,32,256]{3,2,1,0:T(8,128)(2,1)}), bf16[16,4,32,256]{3,2,1,0:T(8,128)(2,1)}, u32[]{:S(2)}, u32[]{:S(2)}) async-start(bf16[16,4,32,256]{3,2,1,0:T(8,128)(2,1)} %copy-done.4), calls=%async_computation.2 | async-start | bytes 2097152 | tf_op jit(solution)/shard_map/all_to_all | solution.py:263
  167.4 0.9 copy-done.8
  168.4 28.9 %shard_map.151 = bf16[16,128,256]{2,1,0:T(8,128)(2,1)S(1)} custom-call(bf16[16,128,256]{2,1,0:T(8,128)(2,1)S(1)} %all-to-all-done.1.q_ref, bf16[16,2,128,256]{3,2,1,0:T(8,128)(2,1)} %all-to-all-done.kv_ref, bf16[512,256]{1,0:T(8,128)(2,1)S(1)} %get-tuple-element.15.key0_ref, bf16[512,256]{1,0:T(8,128)(2,1)S(1)} %copy-done.8), custom_call_target="tpu_custom_call" | custom-call | flops 10737418240 | bytes 4194304 | tf_op jit(solution)/shard_map/pallas_call | solution.py:269
  197.3 0.0 copy-start.3
  197.3 1.0 copy-done.3
  198.3 8.3 %all-to-all-done.2 = bf16[16,4,32,256]{3,2,1,0:T(8,128)(2,1)} async-done(((bf16[16,4,32,256]{3,2,1,0:T(8,128)(2,1)}), bf16[16,4,32,256]{3,2,1,0:T(8,128)(2,1)}, u32[]{:S(2)}, u32[]{:S(2)}) %all-to-all-start.2) | async-done | bytes 1048608 | tf_op jit(solution)/shard_map/all_to_all | solution.py:263
  206.5 10.7 %all-to-all-start.3 = ((bf16[16,128,256]{2,1,0:T(8,128)(2,1)}), bf16[16,128,256]{2,1,0:T(8,128)(2,1)}, u32[]{:S(2)}, u32[]{:S(2)}) async-start(bf16[16,128,256]{2,1,0:T(8,128)(2,1)} %copy-done.3), calls=%async_computation.3 | async-start | bytes 2097152 | tf_op jit(solution)/shard_map/all_to_all | solution.py:289
  217.2 1.6 copy.17
  218.8 1.4 collective-permute-start
  220.2 0.1 dynamic_slice.11
  220.3 1.0 constant_dynamic-slice_fusion.refs_2_
  221.3 19.2 %all-to-all-done.3 = bf16[16,128,256]{2,1,0:T(8,128)(2,1)} async-done(((bf16[16,128,256]{2,1,0:T(8,128)(2,1)}), bf16[16,128,256]{2,1,0:T(8,128)(2,1)}, u32[]{:S(2)}, u32[]{:S(2)}) %all-to-all-start.3) | async-done | bytes 1048608 | tf_op jit(solution)/shard_map/all_to_all | solution.py:289
  240.4 2.3 copy.16
  242.7 2.3 copy.18
  245.0 0.0 collective-permute-done
  245.0 8.5 %convolution_convert_fusion = bf16[128,2048]{1,0:T(8,128)(2,1)S(1)} fusion(bf16[128,4096]{0,1:T(8,128)(2,1)} %collective-permute-done, bf16[4096,2048]{1,0:T(8,128)(2,1)} %all-gather.2.cloned.1.call-done), kind=kOutput, calls=%fused_computation.6 | convolution fusion | flops 2147745792 | bytes 18350080 | tf_op jit(solution)/shard_map/dot_general | solution.py:298
  253.4 1.4 collective-permute-start.1
  254.8 8.1 %convolution_convert_fusion.1.refs_0_ = bf16[128,2048]{1,0:T(8,128)(2,1)S(1)} fusion(bf16[128,4096]{0,1:T(8,128)(2,1)S(1)} %bitcast.19, bf16[4096,2048]{1,0:T(8,128)(2,1)} %all-gather.2.cloned.1.call-done), kind=kOutput, calls=%fused_computation.7 | convolution fusion | flops 2147745792 | bytes 18350080 | tf_op jit(solution)/shard_map/dot_general | solution.py:298
  262.9 4.2 %collective-permute-done.1.refs_1_ = bf16[128,2048]{1,0:T(8,128)(2,1)S(1)} collective-permute-done((bf16[128,2048]{1,0:T(8,128)(2,1)S(1)}, bf16[128,2048]{1,0:T(8,128)(2,1)S(1)}, u32[]{:S(2)}, u32[]{:S(2)}) %collective-permute-start.1) | collective-permute-done | bytes 524320 | tf_op jit(solution)/shard_map/ppermute | solution.py:293
  267.2 0.1 broadcast_in_dim.16.refs_4_
  267.2 2.3 shard_map.152
  (20 shorter events, 0.1 us)
Async XLA Ops:
  7.2 1.6 copy-start
  7.2 237.8 %all-gather.2.cloned.1.call-start = ((), (), s32[]{:S(2)}) async-start(), calls=%async_computation.4 | async-start | bytes 17825792 | tf_op jit(solution)/shard_map/all_gather | solution.py:189
  10.2 13.4 %copy-start.11 = (bf16[4096]{0:T(1024)(128)(2,1)S(1)}, bf16[4096]{0:T(1024)(128)(2,1)}, u32[]{:S(2)}) copy-start(bf16[4096]{0:T(1024)(128)(2,1)} %param.20) | copy-start | bytes 24580
  10.3 14.1 %copy-start.2 = (bf16[128,4096]{1,0:T(8,128)(2,1)S(1)}, bf16[128,4096]{1,0:T(8,128)(2,1)}, u32[]{:S(2)}) copy-start(bf16[128,4096]{1,0:T(8,128)(2,1)} %query_ref.1) | copy-start | bytes 3145732
  10.4 1.3 copy-start.5
  11.7 1.2 copy-start.6
  12.9 17.6 %copy-start.10 = (bf16[4096]{0:T(1024)(128)(2,1)S(1)}, bf16[4096]{0:T(1024)(128)(2,1)}, u32[]{:S(2)}) copy-start(bf16[4096]{0:T(1024)(128)(2,1)} %param.17) | copy-start | bytes 24580
  14.9 1.4 copy-start.1
  16.3 78.3 %all-to-all-start = ((bf16[16,2,128,256]{3,2,1,0:T(8,128)(2,1)}), bf16[16,2,128,256]{3,2,1,0:T(8,128)(2,1)}, u32[]{:S(2)}, u32[]{:S(2)}) async-start(bf16[16,2,128,256]{3,2,1,0:T(8,128)(2,1)} %copy-done.1), calls=%async_computation | async-start | bytes 4194304 | tf_op jit(solution)/shard_map/all_to_all | solution.py:202
  23.6 11.4 %copy-start.9 = (bf16[512,4096]{1,0:T(8,128)(2,1)S(1)}, bf16[512,4096]{1,0:T(8,128)(2,1)}, u32[]{:S(2)}) copy-start(bf16[512,4096]{1,0:T(8,128)(2,1)} %param.16) | copy-start | bytes 12582916
  94.6 53.2 %all-to-all-start.1 = ((bf16[16,128,256]{2,1,0:T(8,128)(2,1)}), bf16[16,128,256]{2,1,0:T(8,128)(2,1)S(1)}, u32[]{:S(2)}, u32[]{:S(2)}) async-start(bf16[16,128,256]{2,1,0:T(8,128)(2,1)} %shard_map.150), calls=%async_computation.1 | async-start | bytes 2097152 | tf_op jit(solution)/shard_map/all_to_all | solution.py:211
  107.5 5.9 %slice-start = ((s8[4325376]{0:T(1024)(128)(4,1)}), s8[4194304]{0:T(1024)(128)(4,1)S(1)}, s32[]{:S(2)}) async-start(s8[4325376]{0:T(1024)(128)(4,1)} %bitcast.20), calls=%async_computation.5 | async-start | bytes 8388608
  109.0 4.4 %slice-start.1 = ((s8[4325376]{0:T(1024)(128)(4,1)}), s8[131072]{0:T(1024)(128)(4,1)S(1)}, s32[]{:S(2)}) async-start(s8[4325376]{0:T(1024)(128)(4,1)} %bitcast.20), calls=%async_computation.6 | async-start | bytes 262144
  109.0 4.4 %copy-start.14 = (bf16[4096,256]{1,0:T(8,128)(2,1)S(1)}, bf16[4096,256]{1,0:T(8,128)(2,1)}, u32[]{:S(2)}) copy-start(bf16[4096,256]{1,0:T(8,128)(2,1)} %param.23) | copy-start | bytes 6291460
  113.4 1.6 copy-start.15
  115.0 1.3 copy-start.13
  134.6 1.0 copy-start.4
  135.6 0.7 copy-start.7
  147.9 58.6 %all-to-all-start.2 = ((bf16[16,4,32,256]{3,2,1,0:T(8,128)(2,1)}), bf16[16,4,32,256]{3,2,1,0:T(8,128)(2,1)}, u32[]{:S(2)}, u32[]{:S(2)}) async-start(bf16[16,4,32,256]{3,2,1,0:T(8,128)(2,1)} %copy-done.4), calls=%async_computation.2 | async-start | bytes 2097152 | tf_op jit(solution)/shard_map/all_to_all | solution.py:263
  167.4 1.0 copy-start.8
  168.4 51.9 %copy-start.12 = (bf16[4096]{0:T(1024)(128)(2,1)S(1)}, bf16[4096]{0:T(1024)(128)(2,1)}, u32[]{:S(2)}) copy-start(bf16[4096]{0:T(1024)(128)(2,1)} %param.21) | copy-start | bytes 24580
  197.3 1.0 copy-start.3
  206.5 33.9 %all-to-all-start.3 = ((bf16[16,128,256]{2,1,0:T(8,128)(2,1)}), bf16[16,128,256]{2,1,0:T(8,128)(2,1)}, u32[]{:S(2)}, u32[]{:S(2)}) async-start(bf16[16,128,256]{2,1,0:T(8,128)(2,1)} %copy-done.3), calls=%async_computation.3 | async-start | bytes 2097152 | tf_op jit(solution)/shard_map/all_to_all | solution.py:289
  218.8 26.1 %collective-permute-start = (bf16[128,4096]{0,1:T(8,128)(2,1)S(1)}, bf16[128,4096]{0,1:T(8,128)(2,1)}, u32[]{:S(2)}, u32[]{:S(2)}) collective-permute-start(bf16[128,4096]{0,1:T(8,128)(2,1)S(1)} %bitcast.18), channel_id=1, source_target_pairs={{0,16},{16,0},{1,17},{17,1},{2,18},{18,2},{3,19},{19,3},{4,20},{20... | collective-permute-start | bytes 3145736 | tf_op jit(solution)/shard_map/ppermute | solution.py:293
  253.4 13.7 %collective-permute-start.1 = (bf16[128,2048]{1,0:T(8,128)(2,1)S(1)}, bf16[128,2048]{1,0:T(8,128)(2,1)S(1)}, u32[]{:S(2)}, u32[]{:S(2)}) collective-permute-start(bf16[128,2048]{1,0:T(8,128)(2,1)S(1)} %convolution_convert_fusion), channel_id=1, source_target_pairs={{0,16},{16,0},{1,17},{17,1},{2,18},{18,2},{3,19},{19,3},{4,20},{20... | collective-permute-start | bytes 1572872 | tf_op jit(solution)/shard_map/ppermute | solution.py:293
Sparse Core Ops, SparseCore 0:
  10.2 209.7 all-gather.1
